TPU v7x, 32 devices: a whole 2x2x4 slice. The times are simulated.
32 devices in a mesh: seq: 16 (over z, y, x), tp: 2 (over core).
Axes of the slice: x: 2, y: 2, z: 4, core: 2. Of those that a mesh axis runs over, the one named last changes fastest.
Arguments:
- residual_in: bfloat16 [2048, 1536], P('seq'), may hold values from -6 to 6
- query_rows: bfloat16 [2048, 2048], P('seq', 'tp'), may hold values from -6 to 6
- rotated_key_rows: bfloat16 [2048, 256], P('seq', 'tp'), may hold values from -6 to 6
- value_row_matrix: bfloat16 [2048, 256], P('seq', 'tp'), may hold values from -6 to 6
- learned_sink_scores: float32 [32], P('tp'), may hold values from 0 to 6
- w_out: bfloat16 [2048, 1536], P('tp'), may hold values from -1 to 1
- norm_gain: float32 [1536], replicated, may hold values from 0.1 to 1.9
- expert_ids: int32 [2048, 4], P('seq'), may hold values from 0 to 15, all different within a row; in each aligned block of 128 rows (0 to 127, 128 to 255, ...) at most 64 rows name the same one
- route_weights: float32 [2048, 4], P('seq'), may hold values from 0.1 to 1
- w_gate: bfloat16 [16, 1536, 1536], P('seq', None, 'tp'), may hold values from -0.15625 to 0.15625
- w_up: bfloat16 [16, 1536, 1536], P('seq', None, 'tp'), may hold values from -0.15625 to 0.15625
- w_down: bfloat16 [16, 1536, 1536], P('seq', 'tp'), may hold values from -0.15625 to 0.15625
Outputs:
- layer_out: bfloat16 [2048, 1536], P('seq', 'tp')
Inputs may be any that keep to these rules, and one draw needn't show every extreme that they name: `expert_ids`: in the rows of one device (aligned blocks of 128 rows) no expert is named by more than 64 rows, and each row names 4 different experts.
All inputs are finite; a program needn't handle non-finite values.
Results may differ from a plain program's by a relative error of at most 0.014.
Values may be sent and summed in bfloat16 or wider, within the bound.
No kernel may reach another device: no remote copies, remote signals or barrier semaphores. Data moves between devices by JAX's collectives and lax.ppermute only.
A program may use at most 64 MiB of HBM per device.

v0:
```python
import functools

import jax
import jax.numpy as jnp
from jax import lax
from jax.experimental import pallas as pl
from jax.experimental.pallas import tpu as pltpu
from jax.sharding import PartitionSpec as P

HEAD_SIZE = 64
WINDOW_LENGTH = 128
LANES = 128
MIB = 1024 * 1024
CUTS = 3
DEEP = 256
AHEAD = 3

neg_large = -1e30
epsilon = 1e-05

VMEM = pl.BlockSpec(memory_space=pltpu.VMEM)
SMEM = pl.BlockSpec(memory_space=pltpu.SMEM)
HBM = pl.BlockSpec(memory_space=pltpu.HBM)


def passed_along(block, axis, distance):
    devices = range(lax.axis_size(axis))
    route = [(i - distance, i) for i in devices if i - distance in devices]
    return lax.ppermute(block, axis, route)


def swapped(block, axis):
    count = lax.axis_size(axis)
    return lax.ppermute(block, axis, [(i, count - 1 - i) for i in range(count)])


def swapped_halves(block, axis):
    count = lax.axis_size(axis)
    return lax.ppermute(block, axis, [(i, (i + count // 2) % count) for i in range(count)])


def shape_of(dims, dtype=jnp.bfloat16):
    return jax.ShapeDtypeStruct(dims, dtype)


def cost(flops, moved, transcendentals=0):
    return pl.CostEstimate(flops=flops, bytes_accessed=moved, transcendentals=transcendentals)


def iota(dims, dimension):
    return lax.broadcasted_iota(jnp.int32, dims, dimension)


def rows_of(ids, experts, side_rows, base, side):
    top_count, tokens = ids.shape
    names = iota((experts, tokens), 0).astype(jnp.float32)
    hits = [ids[c : c + 1, :] == names for c in range(top_count)]
    named = sum([hit.astype(jnp.float32) for hit in hits]).astype(jnp.bfloat16)
    square = (tokens, tokens)
    earlier = (iota(square, 0) < iota(square, 1)).astype(jnp.bfloat16)
    slot = jnp.dot(named, earlier, preferred_element_type=jnp.float32) - (side * side_rows).astype(jnp.float32)
    expert = names - base.astype(jnp.float32)
    here = (slot >= 0.0) & (slot < side_rows) & (expert >= 0.0) & (expert < experts // 2)
    rows = jnp.where(here, expert * side_rows + slot, -1.0)
    lines = [jnp.sum(jnp.where(hit, rows, 0.0), axis=0, keepdims=True) for hit in hits]
    return jnp.concatenate(lines, axis=0).astype(jnp.int32)


def attention_kernel(
    first_ref, sink_ref, q_ref, kv_ref, before_ref, w_hbm, out_ref, w_ref, att_ref, sum_ref, sem
):
    tokens, width = q_ref.shape
    kv_heads = kv_ref.shape[1] // (2 * HEAD_SIZE)
    pairs = width // LANES // kv_heads
    w_load = pltpu.make_async_copy(w_hbm, w_ref, sem)
    w_load.start()
    low = iota((tokens, LANES), 1) < HEAD_SIZE

    def doubled(block, head):
        wide = block.astype(jnp.float32)
        turned = pltpu.roll(wide, HEAD_SIZE, 1)
        first, second = (wide, turned) if head == 0 else (turned, wide)
        return [
            jnp.where(low, first, 0.0).astype(jnp.bfloat16),
            jnp.where(low, 0.0, second).astype(jnp.bfloat16),
        ]

    own = iota((tokens, tokens), 1) <= iota((tokens, tokens), 0)
    bias = jnp.where(own, 0.0, jnp.where(first_ref[0] == 0, 0.0, neg_large))
    own_factor = jnp.where(own, 1.0, 0.0).astype(jnp.bfloat16)
    before_factor = jnp.where(own, 0.0, 1.0).astype(jnp.bfloat16)
    head_lanes = jnp.where(low, 1.0, 0.0).astype(jnp.bfloat16), jnp.where(low, 0.0, 1.0).astype(jnp.bfloat16)
    ones = jnp.concatenate(head_lanes * 2, axis=0)
    keys_before = [jnp.concatenate(doubled(before_ref[:, :LANES], head), axis=0) for head in range(kv_heads)]
    values_before = [doubled(before_ref[:, LANES:], head) for head in range(kv_heads)]
    contract = (((1,), (1,)), ((), ()))
    for head in range(kv_heads):
        keys = jnp.concatenate(doubled(kv_ref[:, :LANES], head), axis=0)
        values = jnp.concatenate(doubled(kv_ref[:, LANES:], head) + values_before[head], axis=0)
        values = jnp.concatenate([values, ones], axis=1)
        for j in range(head * pairs, (head + 1) * pairs):
            q = q_ref[:, j * LANES : (j + 1) * LANES]
            near = lax.dot_general(q, keys, contract, preferred_element_type=jnp.float32)
            far = lax.dot_general(q, keys_before[head], contract, preferred_element_type=jnp.float32)
            terms, sinks = [], []
            for at in range(2):
                span = slice(at * tokens, (at + 1) * tokens)
                part = jnp.where(own, near[:, span], far[:, span]) + bias
                sink = sink_ref[2 * j + at : 2 * j + at + 1, :]
                top = jnp.maximum(jnp.max(part, axis=1, keepdims=True), sink)
                terms.append(jnp.exp(part - top).astype(jnp.bfloat16))
                sinks.append(jnp.exp(sink - top))
            kept = [term * own_factor for term in terms] + [term * before_factor for term in terms]
            found = jnp.dot(jnp.concatenate(kept, axis=1), values, preferred_element_type=jnp.float32)
            total = found[:, LANES:] + jnp.where(low, sinks[0], sinks[1])
            att_ref[:, j * LANES : (j + 1) * LANES] = (found[:, :LANES] / total).astype(jnp.bfloat16)
        if head == 0:
            w_load.wait()
        depth = pairs * LANES
        step = 2 * LANES
        for at in range(0, out_ref.shape[1], step):
            part = jnp.dot(
                att_ref[:, head * depth : (head + 1) * depth],
                w_ref[head * depth : (head + 1) * depth, at : at + step],
                preferred_element_type=jnp.float32,
            )
            if head > 0:
                part += sum_ref[:, at : at + step]
            if head < kv_heads - 1:
                sum_ref[:, at : at + step] = part
            else:
                out_ref[:, at : at + step] = part.astype(jnp.bfloat16)


def attention(first, sinks, q, key_values, before, w_out):
    tokens = q.shape[0]
    return pl.pallas_call(
        attention_kernel,
        out_shape=shape_of((tokens, w_out.shape[1])),
        in_specs=[SMEM, VMEM, VMEM, VMEM, VMEM, HBM],
        out_specs=VMEM,
        scratch_shapes=[
            pltpu.VMEM(w_out.shape, jnp.bfloat16),
            pltpu.VMEM(q.shape, jnp.bfloat16),
            pltpu.VMEM((tokens, w_out.shape[1]), jnp.float32),
            pltpu.SemaphoreType.DMA,
        ],
        compiler_params=pltpu.CompilerParams(vmem_limit_bytes=54_000_000),
        cost_estimate=cost(2 * tokens * w_out.size * 2, 2 * w_out.size, tokens * tokens * q.shape[1] // HEAD_SIZE),
        name="attention",
    )(first, sinks, q, key_values, before, w_out)


def pack(placed, normed, out_ref):
    rows, tokens = out_ref.shape[0], normed.shape[0]
    row = iota((rows, tokens), 0)
    taken = placed[0:1, :] == row
    for c in range(1, placed.shape[0]):
        taken = taken | (placed[c : c + 1, :] == row)
    taken = jnp.where(taken, 1.0, 0.0).astype(jnp.bfloat16)
    out_ref[...] = jnp.dot(taken, normed, preferred_element_type=jnp.float32).astype(jnp.bfloat16)


def norm_kernel(side_ref, residual_ref, near_ref, far_ref, gain_ref, normed_ref, sent_ref, kept_ref, whole_ref):
    side = side_ref[0]
    half_tokens, half = sent_ref.shape[0], kept_ref.shape[1]
    added = near_ref[...].astype(jnp.float32) + far_ref[...].astype(jnp.float32)
    whole = (residual_ref[...].astype(jnp.float32) + added).astype(jnp.bfloat16)
    whole_ref[...] = whole
    wide = whole.astype(jnp.float32)
    mean_square = jnp.mean(wide * wide, axis=1, keepdims=True)
    normed_ref[...] = (wide * lax.rsqrt(mean_square + epsilon) * gain_ref[...]).astype(jnp.bfloat16)
    kept_ref[...] = whole_ref[:, pl.ds(pl.multiple_of(side * half, LANES), half)]
    sent_ref[...] = normed_ref[pl.ds(pl.multiple_of(side * half_tokens, half_tokens), half_tokens), :]


def norm(side, residual_in, near, far, gain, half):
    tokens, width = residual_in.shape
    return pl.pallas_call(
        norm_kernel,
        out_shape=(shape_of((tokens, width)), shape_of((tokens // 2, width)), shape_of((tokens, half))),
        in_specs=[SMEM] + [VMEM] * 4,
        out_specs=(VMEM, VMEM, VMEM),
        scratch_shapes=[pltpu.VMEM((tokens, width), jnp.bfloat16)],
        compiler_params=pltpu.CompilerParams(vmem_limit_bytes=24 * MIB),
        cost_estimate=cost(8 * tokens * width, 10 * tokens * width),
        name="norm",
    )(side, residual_in, near, far, gain.reshape(1, width))


def pack_kernel(experts, side_rows, base_ref, side_ref, notes_ref, *refs):
    *part_refs, out_ref, rows_ref, arrived_ref = refs
    side, top_count = side_ref[0], rows_ref.shape[0]
    if len(part_refs) == 1:
        arrived_ref = part_refs[0]
    else:
        mine_ref, other_ref = part_refs
        part = mine_ref.shape[0]
        arrived_ref[pl.ds(pl.multiple_of(side * part, part), part), :] = mine_ref[...]
        arrived_ref[pl.ds(pl.multiple_of((1 - side) * part, part), part), :] = other_ref[...]
    rows = rows_of(notes_ref[:top_count, :], experts, side_rows, base_ref[0], side)
    rows_ref[...] = rows
    pack(rows, arrived_ref[...], out_ref)


def packed_rows(base, side, notes, parts, experts, side_rows, rows):
    tokens = sum([part.shape[0] for part in parts])
    width = parts[0].shape[1]
    return pl.pallas_call(
        functools.partial(pack_kernel, experts, side_rows),
        out_shape=(shape_of((rows, width)), shape_of((notes.shape[0] // 2, tokens), jnp.int32)),
        in_specs=[SMEM, SMEM, VMEM] + [VMEM] * len(parts),
        out_specs=(VMEM, VMEM),
        scratch_shapes=[pltpu.VMEM((tokens, width), jnp.bfloat16)],
        compiler_params=pltpu.CompilerParams(vmem_limit_bytes=24 * MIB),
        cost_estimate=cost(2 * rows * tokens * width, 2 * rows * width),
        name="packed_rows",
    )(base, side, notes, *parts)


def expert_kernel(
    x_hbm, gate_hbm, up_hbm, down_hbm, gate_too_hbm, up_too_hbm, down_too_hbm, y_hbm, x_ref, y_ref, gate_ref, up_ref,
    down_ref, hidden_ref, gate_sum, up_sum, total_ref, x_sem, y_sem, gate_sem, up_sem, down_sem,
):
    rows, width = x_ref.shape
    share = gate_hbm.shape[2]
    deep, cuts = width // CUTS, share // DEEP
    loads = []
    for k, (gate, up) in enumerate([(gate_hbm, up_hbm), (gate_too_hbm, up_too_hbm)]):
        for c in range(CUTS):
            span = pl.ds(c * deep, deep)
            loads.append(
                [
                    pltpu.make_async_copy(gate.at[0, span], gate_ref.at[k, span], gate_sem.at[k, c]),
                    pltpu.make_async_copy(up.at[0, span], up_ref.at[k, span], up_sem.at[k, c]),
                ]
            )
    for k, down in enumerate([down_hbm, down_too_hbm]):
        for c in range(cuts):
            source, target = pl.ds(c * DEEP, DEEP), pl.ds(k * share + c * DEEP, DEEP)
            loads.append([pltpu.make_async_copy(down.at[0, source], down_ref.at[target], down_sem.at[k, c])])

    def start(number):
        if number < len(loads):
            for load in loads[number]:
                load.start()

    def arrive(number):
        for load in loads[number]:
            load.wait()
        start(number + AHEAD)

    x_load = pltpu.make_async_copy(x_hbm, x_ref, x_sem)
    x_load.start()
    for number in range(AHEAD):
        start(number)
    x_load.wait()
    for k in range(2):
        for c in range(CUTS):
            arrive(k * CUTS + c)
            span = slice(c * deep, (c + 1) * deep)
            x = x_ref[:, span]
            gate = jnp.dot(x, gate_ref[k, span, :], preferred_element_type=jnp.float32)
            up = jnp.dot(x, up_ref[k, span, :], preferred_element_type=jnp.float32)
            if c > 0:
                gate, up = gate_sum[...] + gate, up_sum[...] + up
            if c < CUTS - 1:
                gate_sum[...], up_sum[...] = gate, up
            else:
                hidden = gate * (0.5 + 0.5 * jnp.tanh(0.5 * gate)) * up
                hidden_ref[:, k * share : (k + 1) * share] = hidden.astype(jnp.bfloat16)
    for c in range(2 * cuts - 1):
        arrive(2 * CUTS + c)
        span = slice(c * DEEP, (c + 1) * DEEP)
        part = jnp.dot(hidden_ref[:, span], down_ref[span, :], preferred_element_type=jnp.float32)
        total_ref[...] = part if c == 0 else total_ref[...] + part
    arrive(2 * CUTS + 2 * cuts - 1)
    span = slice((2 * cuts - 1) * DEEP, 2 * cuts * DEEP)
    step = 2 * LANES
    stores = []
    for i in range(width // step):
        columns = slice(i * step, (i + 1) * step)
        part = jnp.dot(hidden_ref[:, span], down_ref[span, columns], preferred_element_type=jnp.float32)
        y_ref[:, columns] = (total_ref[:, columns] + part).astype(jnp.bfloat16)
        column_span = pl.ds(i * step, step)
        stores.append(pltpu.make_async_copy(y_ref.at[:, column_span], y_hbm.at[:, column_span], y_sem.at[i]))
        stores[i].start()
    for store in stores:
        store.wait()


def expert_layer(x, mine, others):
    rows, width = x.shape
    share = mine[0].shape[2]
    return pl.pallas_call(
        expert_kernel,
        out_shape=shape_of((rows, width)),
        in_specs=[HBM] * 7,
        out_specs=HBM,
        scratch_shapes=[
            pltpu.VMEM((rows, width), jnp.bfloat16),
            pltpu.VMEM((rows, width), jnp.bfloat16),
            pltpu.VMEM((2, width, share), jnp.bfloat16),
            pltpu.VMEM((2, width, share), jnp.bfloat16),
            pltpu.VMEM((2 * share, width), jnp.bfloat16),
            pltpu.VMEM((rows, 2 * share), jnp.bfloat16),
            pltpu.VMEM((rows, share), jnp.float32),
            pltpu.VMEM((rows, share), jnp.float32),
            pltpu.VMEM((rows, width), jnp.float32),
            pltpu.SemaphoreType.DMA,
            pltpu.SemaphoreType.DMA((width // (2 * LANES),)),
            pltpu.SemaphoreType.DMA((2, CUTS)),
            pltpu.SemaphoreType.DMA((2, CUTS)),
            pltpu.SemaphoreType.DMA((2, share // DEEP)),
        ],
        compiler_params=pltpu.CompilerParams(vmem_limit_bytes=60 * MIB),
        cost_estimate=cost(12 * rows * width * share, 12 * width * share, 2 * rows * share),
        name="expert_layer",
    )(x, *mine, *others)


def combine_kernel(side_ref, rows_ref, weights_ref, y_ref, *refs):
    *more_refs, mine_ref, sent_ref, total_ref = refs
    top_count, tokens = rows_ref.shape
    half = mine_ref.shape[1]
    row = iota((y_ref.shape[0], tokens), 0)
    share = jnp.zeros(row.shape, jnp.float32)
    for c in range(top_count):
        share = jnp.where(rows_ref[c : c + 1, :] == row, weights_ref[top_count + c : top_count + c + 1, :], share)
    coarse = share.astype(jnp.bfloat16)
    fine = (share - coarse.astype(jnp.float32)).astype(jnp.bfloat16)
    y = y_ref[...]
    contract = (((0,), (0,)), ((), ()))
    total_ref[...] = lax.dot_general(coarse, y, contract, preferred_element_type=jnp.float32)
    total_ref[...] += lax.dot_general(fine, y, contract, preferred_element_type=jnp.float32)
    side = side_ref[0]
    mine = total_ref[:, pl.ds(pl.multiple_of(side * half, LANES), half)]
    for more_ref in more_refs:
        mine += more_ref[...].astype(jnp.float32)
    mine_ref[...] = mine
    sent_ref[...] = total_ref[:, pl.ds(pl.multiple_of((1 - side) * half, LANES), half)].astype(jnp.bfloat16)


def combine(side, placed, weights, y, half, more=()):
    tokens = placed.shape[1]
    rows, width = y.shape
    return pl.pallas_call(
        combine_kernel,
        out_shape=(shape_of((tokens, half), jnp.float32), shape_of((tokens, half))),
        in_specs=[SMEM] + [VMEM] * (3 + len(more)),
        out_specs=(VMEM, VMEM),
        scratch_shapes=[pltpu.VMEM((tokens, width), jnp.float32)],
        compiler_params=pltpu.CompilerParams(vmem_limit_bytes=24 * MIB),
        cost_estimate=cost(4 * rows * tokens * width, 2 * rows * width),
        name="combine",
    )(side, placed, weights, y, *more)


def local(
    residual_in,
    query_rows,
    rotated_key_rows,
    value_row_matrix,
    learned_sink_scores,
    w_out,
    norm_gain,
    expert_ids,
    route_weights,
    w_gate,
    w_up,
    w_down,
):
    tok_dev, model_width = residual_in.shape
    seq_count = lax.axis_size("seq")
    experts = w_gate.shape[0] * seq_count
    capacity = max(2, 8 * tok_dev // experts)
    sides = lax.axis_size("tp")
    side_rows = capacity // sides
    group = seq_count // 2
    rows = experts // 2 * side_rows
    half = model_width // sides
    at_seq = lax.axis_index("seq").astype(jnp.int32)
    base = jnp.where(at_seq < group, 0, experts // 2).astype(jnp.int32).reshape(1)
    side = lax.axis_index("tp").astype(jnp.int32).reshape(1)
    first = (at_seq == 0).astype(jnp.int32).reshape(1)
    key_values = lax.optimization_barrier(jnp.concatenate([rotated_key_rows, value_row_matrix], axis=1))
    before = passed_along(key_values, "seq", 1)
    sinks = jnp.broadcast_to(learned_sink_scores[:, None], (learned_sink_scores.shape[0], LANES))
    sinks, queries = lax.optimization_barrier((sinks, query_rows))
    scaled = queries * jnp.bfloat16(HEAD_SIZE**-0.5)
    weights = (w_gate, w_up, w_down)
    others = [swapped(weight, "tp") for weight in weights[:2]]
    near = attention(
        first, sinks, scaled, key_values, before, w_out
    )
    far, late = lax.optimization_barrier((swapped(near, "tp"), w_down))
    others.append(swapped(late, "tp"))
    normed, sent, kept = norm(side, residual_in, near, far, norm_gain, half)

    def exchanged(block):
        block = block.reshape(group, rows // group, model_width)
        groups = [list(range(group)), list(range(group, seq_count))]
        block = lax.all_to_all(
            block, "seq", split_axis=0, concat_axis=0, axis_index_groups=groups, tiled=True
        )
        return block.reshape(rows, model_width)

    notes = jnp.concatenate([expert_ids.T.astype(jnp.float32), route_weights.T], axis=0)
    crossed = swapped_halves(sent, "seq")
    notes_peer = swapped_halves(notes, "seq")
    packed, placed = packed_rows(base, side, notes, (normed,), experts, side_rows, rows)
    crossed, notes_peer, packed = lax.optimization_barrier((crossed, notes_peer, packed))
    packed_peer, placed_peer = packed_rows(
        base, side, notes_peer, (crossed, swapped(crossed, "tp")), experts, side_rows, rows
    )
    arrived_peer = exchanged(packed_peer)
    arrived_peer, packed, *others = lax.optimization_barrier((arrived_peer, packed, *others))
    arrived = exchanged(packed)
    result_peer = expert_layer(arrived_peer, weights, others)
    result_peer, arrived = lax.optimization_barrier((result_peer, arrived))
    result = expert_layer(arrived, weights, others)

    returned_peer = exchanged(result_peer)
    result, returned_peer = lax.optimization_barrier((result, returned_peer))
    returned = exchanged(result)
    mine_peer, sent_peer = combine(side, placed_peer, notes_peer, returned_peer, half)
    summed_peer = (mine_peer + swapped(sent_peer, "tp").astype(jnp.float32)).astype(jnp.bfloat16)
    back = swapped_halves(summed_peer, "seq")
    mine, sent = combine(side, placed, notes, returned, half, (kept,))
    sent, back = lax.optimization_barrier((sent, back))
    return (mine + swapped(sent, "tp").astype(jnp.float32) + back.astype(jnp.float32)).astype(jnp.bfloat16)


def solution(mesh):
    placed = (
        P("seq", None),
        P("seq", "tp"),
        P("seq", "tp"),
        P("seq", "tp"),
        P("tp"),
        P("tp", None),
        P(),
        P("seq", None),
        P("seq", None),
        P("seq", None, "tp"),
        P("seq", None, "tp"),
        P("seq", "tp", None),
    )
    return jax.shard_map(
        local, mesh=mesh, in_specs=placed, out_specs=P("seq", "tp"), check_vma=False
    )
```

profile of v0, /device:TPU:0, one launch (start us, length us, event | category | flops | bytes accessed | tf_op | source)
XLA Modules:
  0.0 96.7 jit_solution(12793447762391045332)
XLA Ops:
  0.0 0.8 pad_maximum_fusion.kv_ref
  0.8 4.8 %collective-permute-start = (bf16[128,256]{1,0:T(8,128)(2,1)S(1)}, bf16[128,256]{1,0:T(8,128)(2,1)S(1)}, u32[]{:S(2)}, u32[]{:S(2)}) collective-permute-start(bf16[128,256]{1,0:T(8,128)(2,1)S(1)} %pad_maximum_fusion.kv_ref), channel_id=1, source_target_pairs={{0,2},{2,4},{4,6},{6,8},{8,10},{10,12},{12,14},{14,16},{16,18},{18... | collective-permute-start | bytes 196616 | tf_op jit(solution)/shard_map/ppermute | solution.py:29
  5.7 0.7 broadcast_in_dim.2.sink_ref
  6.4 1.0 %broadcast_multiply_fusion.q_ref = bf16[128,1024]{1,0:T(8,128)(2,1)S(1)} fusion(bf16[128,1024]{1,0:T(8,128)(2,1)} %param.13), kind=kLoop, calls=%fused_computation.2 | loop fusion | flops 131072 | bytes 524288 | tf_op jit(solution)/shard_map/mul | solution.py:390
  7.4 0.2 collective-permute-done.before_ref
  7.6 3.1 %attention.1.near_ref = bf16[128,1536]{1,0:T(8,128)(2,1)S(1)} custom-call(s32[1]{0:T(128)} %bitcast.4.first_ref, f32[16,128]{1,0:T(8,128)S(1)} %broadcast_in_dim.2.sink_ref, bf16[128,1024]{1,0:T(8,128)(2,1)S(1)} %broadcast_multiply_fusion.q_ref, bf16[128,256]{1,0:T(8,128)(2,1)S(1)} %pad_maximum_fusion.kv_ref, ...), custom_call_target="tpu_custom_call" | custom-call | flops 805306368 | bytes 3145728 | tf_op jit(solution)/shard_map/attention/pallas_call | solution.py:137
  10.8 0.5 collective-permute-start.5
  11.3 0.1 collective-permute-start.6
  11.4 1.1 %collective-permute-done.1.far_ref = bf16[128,1536]{1,0:T(8,128)(2,1)S(1)} collective-permute-done((bf16[128,1536]{1,0:T(8,128)(2,1)S(1)}, bf16[128,1536]{1,0:T(8,128)(2,1)S(1)}, u32[]{:S(2)}, u32[]{:S(2)}) %collective-permute-start.1) | collective-permute-done | bytes 393248 | tf_op jit(solution)/shard_map/ppermute | solution.py:34
  12.5 0.1 collective-permute-start.7
  12.7 0.4 norm.1
  13.0 5.3 %collective-permute-start.2 = (bf16[64,1536]{1,0:T(8,128)(2,1)S(1)}, bf16[64,1536]{1,0:T(8,128)(2,1)S(1)}, u32[]{:S(2)}, u32[]{:S(2)}) collective-permute-start(bf16[64,1536]{1,0:T(8,128)(2,1)S(1)} %get-tuple-element.39), channel_id=1, source_target_pairs={{0,16},{2,18},{4,20},{6,22},{8,24},{10,26},{12,28},{14,30},{16,0},... | collective-permute-start | bytes 589832 | tf_op jit(solution)/shard_map/ppermute | solution.py:39
  18.4 0.1 collective-permute-start.3
  18.5 1.5 %packed_rows.2 = (bf16[256,1536]{1,0:T(8,128)(2,1)}, s32[4,128]{1,0:T(4,128)S(1)}) custom-call(s32[1]{0:T(128)} %bitcast.1.base_ref, s32[1]{0:T(128)} %bitcast.side_ref, f32[8,128]{1,0:T(8,128)S(1)} %pad_maximum_fusion.1.notes_ref.weights_ref, bf16[128,1536]{1,0:T(8,128)(2,1)S(1)} %get-tuple-element.37.refs_0_), custom_call_target="tpu_custom_call" | custom-call | flops 100663296 | bytes 786432 | tf_op jit(solution)/shard_map/packed_rows/pallas_call | solution.py:209
  20.0 8.2 %collective-permute-done.3.notes_ref.weights_ref = f32[8,128]{1,0:T(8,128)S(1)} collective-permute-done((f32[8,128]{1,0:T(8,128)S(1)}, f32[8,128]{1,0:T(8,128)S(1)}, u32[]{:S(2)}, u32[]{:S(2)}) %collective-permute-start.3) | collective-permute-done | bytes 4128 | tf_op jit(solution)/shard_map/ppermute | solution.py:39
  28.2 1.4 %collective-permute-done.4.refs_1_ = bf16[64,1536]{1,0:T(8,128)(2,1)S(1)} collective-permute-done((bf16[64,1536]{1,0:T(8,128)(2,1)S(1)}, bf16[64,1536]{1,0:T(8,128)(2,1)S(1)}, u32[]{:S(2)}, u32[]{:S(2)}) %collective-permute-start.4) | collective-permute-done | bytes 196640 | tf_op jit(solution)/shard_map/ppermute | solution.py:34
  29.6 0.5 packed_rows.3
  30.1 15.9 %all_to_all.20 = bf16[8,32,1536]{2,1,0:T(8,128)(2,1)} all-to-all(bf16[8,32,1536]{2,1,0:T(8,128)(2,1)S(1)} %bitcast.16), channel_id=1, replica_groups={{0,2,4,6,8,10,12,14},{16,18,20,22,24,26,28,30},{1,3,5,7,9,11,13,15},{17..., dimensions={0} | all-to-all | bytes 1572864 | tf_op jit(solution)/shard_map/all_to_all | solution.py:403
  46.1 3.6 %all-to-all-start.1 = ((bf16[8,32,1536]{2,1,0:T(8,128)(2,1)}), bf16[8,32,1536]{2,1,0:T(8,128)(2,1)S(1)}, u32[]{:S(2)}, u32[]{:S(2)}) async-start(bf16[8,32,1536]{2,1,0:T(8,128)(2,1)} %bitcast.7), calls=%async_computation.1 | async-start | bytes 1572864 | tf_op jit(solution)/shard_map/all_to_all | solution.py:403
  49.6 8.5 %expert_layer.2 = bf16[256,1536]{1,0:T(8,128)(2,1)} custom-call(bf16[256,1536]{1,0:T(8,128)(2,1)} %bitcast.19, bf16[1,1536,768]{2,1,0:T(8,128)(2,1)} %gate_hbm.3, bf16[1,1536,768]{2,1,0:T(8,128)(2,1)} %up_hbm.3, bf16[1,768,1536]{2,1,0:T(8,128)(2,1)} %down_hbm.3, bf16[1,1536,768]{2,1,0:T(8,128)(2,1)} %collective-permute-done.5.gate_too_hbm, ...), custom_call_target="tpu_custom_call" | custom-call | flops 3623878656 | bytes 14155776 | tf_op jit(solution)/shard_map/expert_layer/pallas_call | solution.py:295
  58.1 2.5 %all-to-all-done.1 = bf16[8,32,1536]{2,1,0:T(8,128)(2,1)S(1)} async-done(((bf16[8,32,1536]{2,1,0:T(8,128)(2,1)}), bf16[8,32,1536]{2,1,0:T(8,128)(2,1)S(1)}, u32[]{:S(2)}, u32[]{:S(2)}) %all-to-all-start.1) | async-done | bytes 786464 | tf_op jit(solution)/shard_map/all_to_all | solution.py:403
  60.6 3.5 %all-to-all-start.2 = ((bf16[8,32,1536]{2,1,0:T(8,128)(2,1)}), bf16[8,32,1536]{2,1,0:T(8,128)(2,1)S(1)}, u32[]{:S(2)}, u32[]{:S(2)}) async-start(bf16[8,32,1536]{2,1,0:T(8,128)(2,1)} %bitcast.20), calls=%async_computation.2 | async-start | bytes 1572864 | tf_op jit(solution)/shard_map/all_to_all | solution.py:403
  64.2 8.5 %expert_layer.3 = bf16[256,1536]{1,0:T(8,128)(2,1)} custom-call(bf16[256,1536]{1,0:T(8,128)(2,1)} %bitcast.18, bf16[1,1536,768]{2,1,0:T(8,128)(2,1)} %gate_hbm.3, bf16[1,1536,768]{2,1,0:T(8,128)(2,1)} %up_hbm.3, bf16[1,768,1536]{2,1,0:T(8,128)(2,1)} %down_hbm.3, bf16[1,1536,768]{2,1,0:T(8,128)(2,1)} %collective-permute-done.5.gate_too_hbm, ...), custom_call_target="tpu_custom_call" | custom-call | flops 3623878656 | bytes 14155776 | tf_op jit(solution)/shard_map/expert_layer/pallas_call | solution.py:295
  72.7 2.5 %all-to-all-done.2 = bf16[8,32,1536]{2,1,0:T(8,128)(2,1)S(1)} async-done(((bf16[8,32,1536]{2,1,0:T(8,128)(2,1)}), bf16[8,32,1536]{2,1,0:T(8,128)(2,1)S(1)}, u32[]{:S(2)}, u32[]{:S(2)}) %all-to-all-start.2) | async-done | bytes 786464 | tf_op jit(solution)/shard_map/all_to_all | solution.py:403
  75.2 3.5 %all-to-all-start.3 = ((bf16[8,32,1536]{2,1,0:T(8,128)(2,1)}), bf16[8,32,1536]{2,1,0:T(8,128)(2,1)S(1)}, u32[]{:S(2)}, u32[]{:S(2)}) async-start(bf16[8,32,1536]{2,1,0:T(8,128)(2,1)} %bitcast.17), calls=%async_computation.3 | async-start | bytes 1572864 | tf_op jit(solution)/shard_map/all_to_all | solution.py:403
  78.7 0.5 combine.3
  79.3 1.4 %collective-permute-done.8 = bf16[128,768]{1,0:T(8,128)(2,1)S(1)} collective-permute-done((bf16[128,768]{1,0:T(8,128)(2,1)S(1)}, bf16[128,768]{1,0:T(8,128)(2,1)S(1)}, u32[]{:S(2)}, u32[]{:S(2)}) %collective-permute-start.8) | collective-permute-done | bytes 196640 | tf_op jit(solution)/shard_map/ppermute | solution.py:34
  80.8 1.6 %collective-permute-start.9 = (bf16[128,768]{1,0:T(8,128)(2,1)S(1)}, bf16[128,768]{1,0:T(8,128)(2,1)S(1)}, u32[]{:S(2)}, u32[]{:S(2)}) collective-permute-start(bf16[128,768]{1,0:T(8,128)(2,1)S(1)} %add_convert_fusion.1), channel_id=1, source_target_pairs={{0,16},{2,18},{4,20},{6,22},{8,24},{10,26},{12,28},{14,30},{16,0},... | collective-permute-start | bytes 589832 | tf_op jit(solution)/shard_map/ppermute | solution.py:39
  82.4 11.6 %all-to-all-done.3 = bf16[8,32,1536]{2,1,0:T(8,128)(2,1)S(1)} async-done(((bf16[8,32,1536]{2,1,0:T(8,128)(2,1)}), bf16[8,32,1536]{2,1,0:T(8,128)(2,1)S(1)}, u32[]{:S(2)}, u32[]{:S(2)}) %all-to-all-start.3) | async-done | bytes 786464 | tf_op jit(solution)/shard_map/all_to_all | solution.py:403
  94.0 0.5 combine.2
  94.6 1.4 %collective-permute-done.10 = bf16[128,768]{1,0:T(8,128)(2,1)S(1)} collective-permute-done((bf16[128,768]{1,0:T(8,128)(2,1)S(1)}, bf16[128,768]{1,0:T(8,128)(2,1)S(1)}, u32[]{:S(2)}, u32[]{:S(2)}) %collective-permute-start.10) | collective-permute-done | bytes 196640 | tf_op jit(solution)/shard_map/ppermute | solution.py:34
  96.0 0.7 add_convert_fusion
  (23 shorter events, 0.3 us)
Async XLA Ops:
  0.0 12.6 %copy-start.2 = (f32[1536]{0:T(1024)S(1)}, f32[1536]{0:T(1024)}, u32[]{:S(2)}) copy-start(f32[1536]{0:T(1024)} %param.18) | copy-start | bytes 18436
  0.0 12.6 %copy-start = (bf16[128,1536]{1,0:T(8,128)(2,1)S(1)}, bf16[128,1536]{1,0:T(8,128)(2,1)}, u32[]{:S(2)}) copy-start(bf16[128,1536]{1,0:T(8,128)(2,1)} %residual_ref.1) | copy-start | bytes 1179652
  0.8 6.7 %collective-permute-start = (bf16[128,256]{1,0:T(8,128)(2,1)S(1)}, bf16[128,256]{1,0:T(8,128)(2,1)S(1)}, u32[]{:S(2)}, u32[]{:S(2)}) collective-permute-start(bf16[128,256]{1,0:T(8,128)(2,1)S(1)} %pad_maximum_fusion.kv_ref), channel_id=1, source_target_pairs={{0,2},{2,4},{4,6},{6,8},{8,10},{10,12},{12,14},{14,16},{16,18},{18... | collective-permute-start | bytes 196616 | tf_op jit(solution)/shard_map/ppermute | solution.py:29
  7.6 10.8 %copy-start.3 = (s32[128,4]{0,1:T(4,128)S(1)}, s32[128,4]{0,1:T(4,128)}, u32[]{:S(2)}) copy-start(s32[128,4]{0,1:T(4,128)} %param.19) | copy-start | bytes 6148
  7.6 10.8 %copy-start.4 = (f32[128,4]{0,1:T(4,128)S(1)}, f32[128,4]{0,1:T(4,128)}, u32[]{:S(2)}) copy-start(f32[128,4]{0,1:T(4,128)} %param.20) | copy-start | bytes 6148
  10.7 1.8 %collective-permute-start.1 = (bf16[128,1536]{1,0:T(8,128)(2,1)S(1)}, bf16[128,1536]{1,0:T(8,128)(2,1)S(1)}, u32[]{:S(2)}, u32[]{:S(2)}) collective-permute-start(bf16[128,1536]{1,0:T(8,128)(2,1)S(1)} %attention.1.near_ref), channel_id=1, source_target_pairs={{0,1},{1,0},{2,3},{3,2},{4,5},{5,4},{6,7},{7,6},{8,9},{9,8},{10,11... | collective-permute-start | bytes 1179656 | tf_op jit(solution)/shard_map/ppermute | solution.py:34
  10.8 35.3 %collective-permute-start.5 = (bf16[1,1536,768]{2,1,0:T(8,128)(2,1)}, bf16[1,1536,768]{2,1,0:T(8,128)(2,1)}, u32[]{:S(2)}, u32[]{:S(2)}) collective-permute-start(bf16[1,1536,768]{2,1,0:T(8,128)(2,1)} %gate_hbm.3), channel_id=1, source_target_pairs={{0,1},{1,0},{2,3},{3,2},{4,5},{5,4},{6,7},{7,6},{8,9},{9,8},{10,11... | collective-permute-start | bytes 7077896 | tf_op jit(solution)/shard_map/ppermute | solution.py:34
  11.3 34.8 %collective-permute-start.6 = (bf16[1,1536,768]{2,1,0:T(8,128)(2,1)}, bf16[1,1536,768]{2,1,0:T(8,128)(2,1)}, u32[]{:S(2)}, u32[]{:S(2)}) collective-permute-start(bf16[1,1536,768]{2,1,0:T(8,128)(2,1)} %up_hbm.3), channel_id=1, source_target_pairs={{0,1},{1,0},{2,3},{3,2},{4,5},{5,4},{6,7},{7,6},{8,9},{9,8},{10,11... | collective-permute-start | bytes 7077896 | tf_op jit(solution)/shard_map/ppermute | solution.py:34
  12.5 33.6 %collective-permute-start.7 = (bf16[1,768,1536]{2,1,0:T(8,128)(2,1)}, bf16[1,768,1536]{2,1,0:T(8,128)(2,1)}, u32[]{:S(2)}, u32[]{:S(2)}) collective-permute-start(bf16[1,768,1536]{2,1,0:T(8,128)(2,1)} %down_hbm.3), channel_id=1, source_target_pairs={{0,1},{1,0},{2,3},{3,2},{4,5},{5,4},{6,7},{7,6},{8,9},{9,8},{10,11... | collective-permute-start | bytes 7077896 | tf_op jit(solution)/shard_map/ppermute | solution.py:34
  13.0 15.2 %collective-permute-start.2 = (bf16[64,1536]{1,0:T(8,128)(2,1)S(1)}, bf16[64,1536]{1,0:T(8,128)(2,1)S(1)}, u32[]{:S(2)}, u32[]{:S(2)}) collective-permute-start(bf16[64,1536]{1,0:T(8,128)(2,1)S(1)} %get-tuple-element.39), channel_id=1, source_target_pairs={{0,16},{2,18},{4,20},{6,22},{8,24},{10,26},{12,28},{14,30},{16,0},... | collective-permute-start | bytes 589832 | tf_op jit(solution)/shard_map/ppermute | solution.py:39
  18.4 9.8 %collective-permute-start.3 = (f32[8,128]{1,0:T(8,128)S(1)}, f32[8,128]{1,0:T(8,128)S(1)}, u32[]{:S(2)}, u32[]{:S(2)}) collective-permute-start(f32[8,128]{1,0:T(8,128)S(1)} %pad_maximum_fusion.1.notes_ref.weights_ref), channel_id=1, source_target_pairs={{0,16},{2,18},{4,20},{6,22},{8,24},{10,26},{12,28},{14,30},{16,0},... | collective-permute-start | bytes 12296 | tf_op jit(solution)/shard_map/ppermute | solution.py:39
  28.2 1.4 %collective-permute-start.4 = (bf16[64,1536]{1,0:T(8,128)(2,1)S(1)}, bf16[64,1536]{1,0:T(8,128)(2,1)S(1)}, u32[]{:S(2)}, u32[]{:S(2)}) collective-permute-start(bf16[64,1536]{1,0:T(8,128)(2,1)S(1)} %collective-permute-done.2.refs_0_), channel_id=1, source_target_pairs={{0,1},{1,0},{2,3},{3,2},{4,5},{5,4},{6,7},{7,6},{8,9},{9,8},{10,11... | collective-permute-start | bytes 589832 | tf_op jit(solution)/shard_map/ppermute | solution.py:34
  46.1 14.5 %all-to-all-start.1 = ((bf16[8,32,1536]{2,1,0:T(8,128)(2,1)}), bf16[8,32,1536]{2,1,0:T(8,128)(2,1)S(1)}, u32[]{:S(2)}, u32[]{:S(2)}) async-start(bf16[8,32,1536]{2,1,0:T(8,128)(2,1)} %bitcast.7), calls=%async_computation.1 | async-start | bytes 1572864 | tf_op jit(solution)/shard_map/all_to_all | solution.py:403
  60.6 3.6 %copy-start.1 = (bf16[8,32,1536]{2,1,0:T(8,128)(2,1)}, bf16[8,32,1536]{2,1,0:T(8,128)(2,1)S(1)}, u32[]{:S(2)}) copy-start(bf16[8,32,1536]{2,1,0:T(8,128)(2,1)S(1)} %all-to-all-done.1) | copy-start | bytes 2359300
  60.6 14.6 %all-to-all-start.2 = ((bf16[8,32,1536]{2,1,0:T(8,128)(2,1)}), bf16[8,32,1536]{2,1,0:T(8,128)(2,1)S(1)}, u32[]{:S(2)}, u32[]{:S(2)}) async-start(bf16[8,32,1536]{2,1,0:T(8,128)(2,1)} %bitcast.20), calls=%async_computation.2 | async-start | bytes 1572864 | tf_op jit(solution)/shard_map/all_to_all | solution.py:403
  75.2 18.8 %all-to-all-start.3 = ((bf16[8,32,1536]{2,1,0:T(8,128)(2,1)}), bf16[8,32,1536]{2,1,0:T(8,128)(2,1)S(1)}, u32[]{:S(2)}, u32[]{:S(2)}) async-start(bf16[8,32,1536]{2,1,0:T(8,128)(2,1)} %bitcast.17), calls=%async_computation.3 | async-start | bytes 1572864 | tf_op jit(solution)/shard_map/all_to_all | solution.py:403
  79.2 1.5 %collective-permute-start.8 = (bf16[128,768]{1,0:T(8,128)(2,1)S(1)}, bf16[128,768]{1,0:T(8,128)(2,1)S(1)}, u32[]{:S(2)}, u32[]{:S(2)}) collective-permute-start(bf16[128,768]{1,0:T(8,128)(2,1)S(1)} %get-tuple-element.60), channel_id=1, source_target_pairs={{0,1},{1,0},{2,3},{3,2},{4,5},{5,4},{6,7},{7,6},{8,9},{9,8},{10,11... | collective-permute-start | bytes 589832 | tf_op jit(solution)/shard_map/ppermute | solution.py:34
  80.8 13.7 %collective-permute-start.9 = (bf16[128,768]{1,0:T(8,128)(2,1)S(1)}, bf16[128,768]{1,0:T(8,128)(2,1)S(1)}, u32[]{:S(2)}, u32[]{:S(2)}) collective-permute-start(bf16[128,768]{1,0:T(8,128)(2,1)S(1)} %add_convert_fusion.1), channel_id=1, source_target_pairs={{0,16},{2,18},{4,20},{6,22},{8,24},{10,26},{12,28},{14,30},{16,0},... | collective-permute-start | bytes 589832 | tf_op jit(solution)/shard_map/ppermute | solution.py:39
  94.5 1.5 %collective-permute-start.10 = (bf16[128,768]{1,0:T(8,128)(2,1)S(1)}, bf16[128,768]{1,0:T(8,128)(2,1)S(1)}, u32[]{:S(2)}, u32[]{:S(2)}) collective-permute-start(bf16[128,768]{1,0:T(8,128)(2,1)S(1)} %get-tuple-element.61), channel_id=1, source_target_pairs={{0,1},{1,0},{2,3},{3,2},{4,5},{5,4},{6,7},{7,6},{8,9},{9,8},{10,11... | collective-permute-start | bytes 589832 | tf_op jit(solution)/shard_map/ppermute | solution.py:34
where the time goes:
time: 97.3 us; the launch traced here: 96.7 us
  waiting for transfers between devices  30.3 us (31%)
  starting transfers between devices  23.5 us (24%)
  Pallas kernels  23.5 us (24%)
  blocking collectives  15.9 us (16%)
  other arithmetic  2.61 us (3%)
    pallas_call x2, Pallas kernels, expert_layer(): pl.pallas_call(expert_kernel, out_shape=shape_of((rows, width)), in_specs...  17 us
    all_to_all x3, waiting for transfers between devices, exchanged(): lax.all_to_all(block, 'seq', split_axis=0, concat_axis=0, axis_index_grou...  16.5 us
    all_to_all x1, blocking collectives, exchanged(): lax.all_to_all(block, 'seq', split_axis=0, concat_axis=0, axis_index_grou...  15.9 us
    all_to_all x3, starting transfers between devices, exchanged(): lax.all_to_all(block, 'seq', split_axis=0, concat_axis=0, axis_index_grou...  10.7 us
    ppermute x3, waiting for transfers between devices, swapped_halves(): lax.ppermute(block, axis, [(i, (i + count // 2) % count) for i in range(c...  8.22 us
    ppermute x3, starting transfers between devices, swapped_halves(): lax.ppermute(block, axis, [(i, (i + count // 2) % count) for i in range(c...  7.09 us
    ppermute x7, waiting for transfers between devices, swapped(): return lax.ppermute(block, axis, [(i, count - 1 - i) for i in range(count)])  5.44 us
    ppermute x1, starting transfers between devices, passed_along(): return lax.ppermute(block, axis, route)  4.84 us
  transfers between devices with their start and end apart: 14, of which 9 were waited for; matrix products, arithmetic and copies ran while one was open for 2% of the time, Pallas kernels for 21%

commit v1 on v0

--- a/solution.py
+++ b/solution.py
@@ -15,7 +15,6 @@
 DEEP = 256
 AHEAD = 3
 
-neg_large = -1e30
 epsilon = 1e-05
 
 VMEM = pl.BlockSpec(memory_space=pltpu.VMEM)
@@ -67,13 +66,16 @@
 
 
 def attention_kernel(
-    first_ref, sink_ref, q_ref, kv_ref, before_ref, w_hbm, out_ref, w_ref, att_ref, sum_ref, sem
+    first_ref, sink_ref, q_ref, kv_ref, before_ref, w_hbm, out_ref, w_ref, att_ref, sum_ref, sems
 ):
     tokens, width = q_ref.shape
     kv_heads = kv_ref.shape[1] // (2 * HEAD_SIZE)
     pairs = width // LANES // kv_heads
-    w_load = pltpu.make_async_copy(w_hbm, w_ref, sem)
-    w_load.start()
+    depth = pairs * LANES
+    spans = [pl.ds(head * depth, depth) for head in range(kv_heads)]
+    w_loads = [pltpu.make_async_copy(w_hbm.at[span], w_ref.at[span], sems.at[i]) for i, span in enumerate(spans)]
+    for load in w_loads:
+        load.start()
     low = iota((tokens, LANES), 1) < HEAD_SIZE
 
     def doubled(block, head):
@@ -86,9 +88,9 @@
         ]
 
     own = iota((tokens, tokens), 1) <= iota((tokens, tokens), 0)
-    bias = jnp.where(own, 0.0, jnp.where(first_ref[0] == 0, 0.0, neg_large))
+    usable = jnp.where(first_ref[0] == 0, 1.0, 0.0)
     own_factor = jnp.where(own, 1.0, 0.0).astype(jnp.bfloat16)
-    before_factor = jnp.where(own, 0.0, 1.0).astype(jnp.bfloat16)
+    before_factor = jnp.where(own, 0.0, usable).astype(jnp.bfloat16)
     head_lanes = jnp.where(low, 1.0, 0.0).astype(jnp.bfloat16), jnp.where(low, 0.0, 1.0).astype(jnp.bfloat16)
     ones = jnp.concatenate(head_lanes * 2, axis=0)
     keys_before = [jnp.concatenate(doubled(before_ref[:, :LANES], head), axis=0) for head in range(kv_heads)]
@@ -105,7 +107,7 @@
             terms, sinks = [], []
             for at in range(2):
                 span = slice(at * tokens, (at + 1) * tokens)
-                part = jnp.where(own, near[:, span], far[:, span]) + bias
+                part = jnp.where(own, near[:, span], far[:, span])
                 sink = sink_ref[2 * j + at : 2 * j + at + 1, :]
                 top = jnp.maximum(jnp.max(part, axis=1, keepdims=True), sink)
                 terms.append(jnp.exp(part - top).astype(jnp.bfloat16))
@@ -114,9 +116,7 @@
             found = jnp.dot(jnp.concatenate(kept, axis=1), values, preferred_element_type=jnp.float32)
             total = found[:, LANES:] + jnp.where(low, sinks[0], sinks[1])
             att_ref[:, j * LANES : (j + 1) * LANES] = (found[:, :LANES] / total).astype(jnp.bfloat16)
-        if head == 0:
-            w_load.wait()
-        depth = pairs * LANES
+        w_loads[head].wait()
         step = 2 * LANES
         for at in range(0, out_ref.shape[1], step):
             part = jnp.dot(
@@ -143,7 +143,7 @@
             pltpu.VMEM(w_out.shape, jnp.bfloat16),
             pltpu.VMEM(q.shape, jnp.bfloat16),
             pltpu.VMEM((tokens, w_out.shape[1]), jnp.float32),
-            pltpu.SemaphoreType.DMA,
+            pltpu.SemaphoreType.DMA((key_values.shape[1] // (2 * HEAD_SIZE),)),
         ],
         compiler_params=pltpu.CompilerParams(vmem_limit_bytes=54_000_000),
         cost_estimate=cost(2 * tokens * w_out.size * 2, 2 * w_out.size, tokens * tokens * q.shape[1] // HEAD_SIZE),

time: 97.3 us -> 96.9 us (level)
  no operation moved by 1% of the time
where the time goes in v1:
time: 96.9 us; the launch traced here: 96.3 us
  waiting for transfers between devices  30.3 us (31%)
  starting transfers between devices  23.5 us (24%)
  Pallas kernels  23.1 us (24%)
  blocking collectives  15.9 us (16%)
  other arithmetic  2.61 us (3%)
    pallas_call x2, Pallas kernels, expert_layer(): pl.pallas_call(expert_kernel, out_shape=shape_of((rows, width)), in_specs...  17 us
    all_to_all x3, waiting for transfers between devices, exchanged(): lax.all_to_all(block, 'seq', split_axis=0, concat_axis=0, axis_index_grou...  16.5 us
    all_to_all x1, blocking collectives, exchanged(): lax.all_to_all(block, 'seq', split_axis=0, concat_axis=0, axis_index_grou...  15.9 us
    all_to_all x3, starting transfers between devices, exchanged(): lax.all_to_all(block, 'seq', split_axis=0, concat_axis=0, axis_index_grou...  10.7 us
    ppermute x3, waiting for transfers between devices, swapped_halves(): lax.ppermute(block, axis, [(i, (i + count // 2) % count) for i in range(c...  8.22 us
    ppermute x3, starting transfers between devices, swapped_halves(): lax.ppermute(block, axis, [(i, (i + count // 2) % count) for i in range(c...  7.1 us
    ppermute x7, waiting for transfers between devices, swapped(): return lax.ppermute(block, axis, [(i, count - 1 - i) for i in range(count)])  5.44 us
    ppermute x1, starting transfers between devices, passed_along(): return lax.ppermute(block, axis, route)  4.84 us
  transfers between devices with their start and end apart: 14, of which 9 were waited for; matrix products, arithmetic and copies ran while one was open for 2% of the time, Pallas kernels for 21%

profile of v1, /device:TPU:0, one launch (start us, length us, event | category | flops | bytes accessed | tf_op | source)
XLA Modules:
  0.0 96.3 jit_solution(921956455192887418)
XLA Ops:
  0.0 0.8 pad_maximum_fusion.kv_ref
  0.8 4.8 %collective-permute-start = (bf16[128,256]{1,0:T(8,128)(2,1)S(1)}, bf16[128,256]{1,0:T(8,128)(2,1)S(1)}, u32[]{:S(2)}, u32[]{:S(2)}) collective-permute-start(bf16[128,256]{1,0:T(8,128)(2,1)S(1)} %pad_maximum_fusion.kv_ref), channel_id=1, source_target_pairs={{0,2},{2,4},{4,6},{6,8},{8,10},{10,12},{12,14},{14,16},{16,18},{18... | collective-permute-start | bytes 196616 | tf_op jit(solution)/shard_map/ppermute | solution.py:28
  5.7 0.7 broadcast_in_dim.2.sink_ref
  6.4 1.0 %broadcast_multiply_fusion.q_ref = bf16[128,1024]{1,0:T(8,128)(2,1)S(1)} fusion(bf16[128,1024]{1,0:T(8,128)(2,1)} %param.13), kind=kLoop, calls=%fused_computation.2 | loop fusion | flops 131072 | bytes 524288 | tf_op jit(solution)/shard_map/mul | solution.py:390
  7.4 0.2 collective-permute-done.before_ref
  7.6 2.7 %attention.1.near_ref = bf16[128,1536]{1,0:T(8,128)(2,1)S(1)} custom-call(s32[1]{0:T(128)} %bitcast.4.first_ref, f32[16,128]{1,0:T(8,128)S(1)} %broadcast_in_dim.2.sink_ref, bf16[128,1024]{1,0:T(8,128)(2,1)S(1)} %broadcast_multiply_fusion.q_ref, bf16[128,256]{1,0:T(8,128)(2,1)S(1)} %pad_maximum_fusion.kv_ref, ...), custom_call_target="tpu_custom_call" | custom-call | flops 805306368 | bytes 3145728 | tf_op jit(solution)/shard_map/attention/pallas_call | solution.py:137
  10.4 0.5 collective-permute-start.5
  10.9 0.1 collective-permute-start.6
  11.0 1.1 %collective-permute-done.1.far_ref = bf16[128,1536]{1,0:T(8,128)(2,1)S(1)} collective-permute-done((bf16[128,1536]{1,0:T(8,128)(2,1)S(1)}, bf16[128,1536]{1,0:T(8,128)(2,1)S(1)}, u32[]{:S(2)}, u32[]{:S(2)}) %collective-permute-start.1) | collective-permute-done | bytes 393248 | tf_op jit(solution)/shard_map/ppermute | solution.py:33
  12.1 0.1 collective-permute-start.7
  12.3 0.4 norm.1
  12.6 5.3 %collective-permute-start.2 = (bf16[64,1536]{1,0:T(8,128)(2,1)S(1)}, bf16[64,1536]{1,0:T(8,128)(2,1)S(1)}, u32[]{:S(2)}, u32[]{:S(2)}) collective-permute-start(bf16[64,1536]{1,0:T(8,128)(2,1)S(1)} %get-tuple-element.39), channel_id=1, source_target_pairs={{0,16},{2,18},{4,20},{6,22},{8,24},{10,26},{12,28},{14,30},{16,0},... | collective-permute-start | bytes 589832 | tf_op jit(solution)/shard_map/ppermute | solution.py:38
  18.0 0.1 collective-permute-start.3
  18.1 1.5 %packed_rows.2 = (bf16[256,1536]{1,0:T(8,128)(2,1)}, s32[4,128]{1,0:T(4,128)S(1)}) custom-call(s32[1]{0:T(128)} %bitcast.1.base_ref, s32[1]{0:T(128)} %bitcast.side_ref, f32[8,128]{1,0:T(8,128)S(1)} %pad_maximum_fusion.1.notes_ref.weights_ref, bf16[128,1536]{1,0:T(8,128)(2,1)S(1)} %get-tuple-element.37.refs_0_), custom_call_target="tpu_custom_call" | custom-call | flops 100663296 | bytes 786432 | tf_op jit(solution)/shard_map/packed_rows/pallas_call | solution.py:209
  19.6 8.2 %collective-permute-done.3.notes_ref.weights_ref = f32[8,128]{1,0:T(8,128)S(1)} collective-permute-done((f32[8,128]{1,0:T(8,128)S(1)}, f32[8,128]{1,0:T(8,128)S(1)}, u32[]{:S(2)}, u32[]{:S(2)}) %collective-permute-start.3) | collective-permute-done | bytes 4128 | tf_op jit(solution)/shard_map/ppermute | solution.py:38
  27.8 1.4 %collective-permute-done.4.refs_1_ = bf16[64,1536]{1,0:T(8,128)(2,1)S(1)} collective-permute-done((bf16[64,1536]{1,0:T(8,128)(2,1)S(1)}, bf16[64,1536]{1,0:T(8,128)(2,1)S(1)}, u32[]{:S(2)}, u32[]{:S(2)}) %collective-permute-start.4) | collective-permute-done | bytes 196640 | tf_op jit(solution)/shard_map/ppermute | solution.py:33
  29.2 0.5 packed_rows.3
  29.7 15.9 %all_to_all.20 = bf16[8,32,1536]{2,1,0:T(8,128)(2,1)} all-to-all(bf16[8,32,1536]{2,1,0:T(8,128)(2,1)S(1)} %bitcast.16), channel_id=1, replica_groups={{0,2,4,6,8,10,12,14},{16,18,20,22,24,26,28,30},{1,3,5,7,9,11,13,15},{17..., dimensions={0} | all-to-all | bytes 1572864 | tf_op jit(solution)/shard_map/all_to_all | solution.py:403
  45.7 3.6 %all-to-all-start.1 = ((bf16[8,32,1536]{2,1,0:T(8,128)(2,1)}), bf16[8,32,1536]{2,1,0:T(8,128)(2,1)S(1)}, u32[]{:S(2)}, u32[]{:S(2)}) async-start(bf16[8,32,1536]{2,1,0:T(8,128)(2,1)} %bitcast.7), calls=%async_computation.1 | async-start | bytes 1572864 | tf_op jit(solution)/shard_map/all_to_all | solution.py:403
  49.2 8.5 %expert_layer.2 = bf16[256,1536]{1,0:T(8,128)(2,1)} custom-call(bf16[256,1536]{1,0:T(8,128)(2,1)} %bitcast.19, bf16[1,1536,768]{2,1,0:T(8,128)(2,1)} %gate_hbm.3, bf16[1,1536,768]{2,1,0:T(8,128)(2,1)} %up_hbm.3, bf16[1,768,1536]{2,1,0:T(8,128)(2,1)} %down_hbm.3, bf16[1,1536,768]{2,1,0:T(8,128)(2,1)} %collective-permute-done.5.gate_too_hbm, ...), custom_call_target="tpu_custom_call" | custom-call | flops 3623878656 | bytes 14155776 | tf_op jit(solution)/shard_map/expert_layer/pallas_call | solution.py:295
  57.7 2.5 %all-to-all-done.1 = bf16[8,32,1536]{2,1,0:T(8,128)(2,1)S(1)} async-done(((bf16[8,32,1536]{2,1,0:T(8,128)(2,1)}), bf16[8,32,1536]{2,1,0:T(8,128)(2,1)S(1)}, u32[]{:S(2)}, u32[]{:S(2)}) %all-to-all-start.1) | async-done | bytes 786464 | tf_op jit(solution)/shard_map/all_to_all | solution.py:403
  60.2 3.5 %all-to-all-start.2 = ((bf16[8,32,1536]{2,1,0:T(8,128)(2,1)}), bf16[8,32,1536]{2,1,0:T(8,128)(2,1)S(1)}, u32[]{:S(2)}, u32[]{:S(2)}) async-start(bf16[8,32,1536]{2,1,0:T(8,128)(2,1)} %bitcast.20), calls=%async_computation.2 | async-start | bytes 1572864 | tf_op jit(solution)/shard_map/all_to_all | solution.py:403
  63.8 8.5 %expert_layer.3 = bf16[256,1536]{1,0:T(8,128)(2,1)} custom-call(bf16[256,1536]{1,0:T(8,128)(2,1)} %bitcast.18, bf16[1,1536,768]{2,1,0:T(8,128)(2,1)} %gate_hbm.3, bf16[1,1536,768]{2,1,0:T(8,128)(2,1)} %up_hbm.3, bf16[1,768,1536]{2,1,0:T(8,128)(2,1)} %down_hbm.3, bf16[1,1536,768]{2,1,0:T(8,128)(2,1)} %collective-permute-done.5.gate_too_hbm, ...), custom_call_target="tpu_custom_call" | custom-call | flops 3623878656 | bytes 14155776 | tf_op jit(solution)/shard_map/expert_layer/pallas_call | solution.py:295
  72.3 2.5 %all-to-all-done.2 = bf16[8,32,1536]{2,1,0:T(8,128)(2,1)S(1)} async-done(((bf16[8,32,1536]{2,1,0:T(8,128)(2,1)}), bf16[8,32,1536]{2,1,0:T(8,128)(2,1)S(1)}, u32[]{:S(2)}, u32[]{:S(2)}) %all-to-all-start.2) | async-done | bytes 786464 | tf_op jit(solution)/shard_map/all_to_all | solution.py:403
  74.8 3.5 %all-to-all-start.3 = ((bf16[8,32,1536]{2,1,0:T(8,128)(2,1)}), bf16[8,32,1536]{2,1,0:T(8,128)(2,1)S(1)}, u32[]{:S(2)}, u32[]{:S(2)}) async-start(bf16[8,32,1536]{2,1,0:T(8,128)(2,1)} %bitcast.17), calls=%async_computation.3 | async-start | bytes 1572864 | tf_op jit(solution)/shard_map/all_to_all | solution.py:403
  78.3 0.5 combine.3
  78.9 1.4 %collective-permute-done.8 = bf16[128,768]{1,0:T(8,128)(2,1)S(1)} collective-permute-done((bf16[128,768]{1,0:T(8,128)(2,1)S(1)}, bf16[128,768]{1,0:T(8,128)(2,1)S(1)}, u32[]{:S(2)}, u32[]{:S(2)}) %collective-permute-start.8) | collective-permute-done | bytes 196640 | tf_op jit(solution)/shard_map/ppermute | solution.py:33
  80.4 1.7 %collective-permute-start.9 = (bf16[128,768]{1,0:T(8,128)(2,1)S(1)}, bf16[128,768]{1,0:T(8,128)(2,1)S(1)}, u32[]{:S(2)}, u32[]{:S(2)}) collective-permute-start(bf16[128,768]{1,0:T(8,128)(2,1)S(1)} %add_convert_fusion.1), channel_id=1, source_target_pairs={{0,16},{2,18},{4,20},{6,22},{8,24},{10,26},{12,28},{14,30},{16,0},... | collective-permute-start | bytes 589832 | tf_op jit(solution)/shard_map/ppermute | solution.py:38
  82.0 11.6 %all-to-all-done.3 = bf16[8,32,1536]{2,1,0:T(8,128)(2,1)S(1)} async-done(((bf16[8,32,1536]{2,1,0:T(8,128)(2,1)}), bf16[8,32,1536]{2,1,0:T(8,128)(2,1)S(1)}, u32[]{:S(2)}, u32[]{:S(2)}) %all-to-all-start.3) | async-done | bytes 786464 | tf_op jit(solution)/shard_map/all_to_all | solution.py:403
  93.6 0.5 combine.2
  94.2 1.4 %collective-permute-done.10 = bf16[128,768]{1,0:T(8,128)(2,1)S(1)} collective-permute-done((bf16[128,768]{1,0:T(8,128)(2,1)S(1)}, bf16[128,768]{1,0:T(8,128)(2,1)S(1)}, u32[]{:S(2)}, u32[]{:S(2)}) %collective-permute-start.10) | collective-permute-done | bytes 196640 | tf_op jit(solution)/shard_map/ppermute | solution.py:33
  95.6 0.7 add_convert_fusion
  (23 shorter events, 0.3 us)
Async XLA Ops:
  0.0 12.2 %copy-start.2 = (f32[1536]{0:T(1024)S(1)}, f32[1536]{0:T(1024)}, u32[]{:S(2)}) copy-start(f32[1536]{0:T(1024)} %param.18) | copy-start | bytes 18436
  0.0 12.3 %copy-start = (bf16[128,1536]{1,0:T(8,128)(2,1)S(1)}, bf16[128,1536]{1,0:T(8,128)(2,1)}, u32[]{:S(2)}) copy-start(bf16[128,1536]{1,0:T(8,128)(2,1)} %residual_ref.1) | copy-start | bytes 1179652
  0.8 6.7 %collective-permute-start = (bf16[128,256]{1,0:T(8,128)(2,1)S(1)}, bf16[128,256]{1,0:T(8,128)(2,1)S(1)}, u32[]{:S(2)}, u32[]{:S(2)}) collective-permute-start(bf16[128,256]{1,0:T(8,128)(2,1)S(1)} %pad_maximum_fusion.kv_ref), channel_id=1, source_target_pairs={{0,2},{2,4},{4,6},{6,8},{8,10},{10,12},{12,14},{14,16},{16,18},{18... | collective-permute-start | bytes 196616 | tf_op jit(solution)/shard_map/ppermute | solution.py:28
  7.6 10.4 %copy-start.3 = (s32[128,4]{0,1:T(4,128)S(1)}, s32[128,4]{0,1:T(4,128)}, u32[]{:S(2)}) copy-start(s32[128,4]{0,1:T(4,128)} %param.19) | copy-start | bytes 6148
  7.6 10.4 %copy-start.4 = (f32[128,4]{0,1:T(4,128)S(1)}, f32[128,4]{0,1:T(4,128)}, u32[]{:S(2)}) copy-start(f32[128,4]{0,1:T(4,128)} %param.20) | copy-start | bytes 6148
  10.3 1.8 %collective-permute-start.1 = (bf16[128,1536]{1,0:T(8,128)(2,1)S(1)}, bf16[128,1536]{1,0:T(8,128)(2,1)S(1)}, u32[]{:S(2)}, u32[]{:S(2)}) collective-permute-start(bf16[128,1536]{1,0:T(8,128)(2,1)S(1)} %attention.1.near_ref), channel_id=1, source_target_pairs={{0,1},{1,0},{2,3},{3,2},{4,5},{5,4},{6,7},{7,6},{8,9},{9,8},{10,11... | collective-permute-start | bytes 1179656 | tf_op jit(solution)/shard_map/ppermute | solution.py:33
  10.4 35.3 %collective-permute-start.5 = (bf16[1,1536,768]{2,1,0:T(8,128)(2,1)}, bf16[1,1536,768]{2,1,0:T(8,128)(2,1)}, u32[]{:S(2)}, u32[]{:S(2)}) collective-permute-start(bf16[1,1536,768]{2,1,0:T(8,128)(2,1)} %gate_hbm.3), channel_id=1, source_target_pairs={{0,1},{1,0},{2,3},{3,2},{4,5},{5,4},{6,7},{7,6},{8,9},{9,8},{10,11... | collective-permute-start | bytes 7077896 | tf_op jit(solution)/shard_map/ppermute | solution.py:33
  10.9 34.8 %collective-permute-start.6 = (bf16[1,1536,768]{2,1,0:T(8,128)(2,1)}, bf16[1,1536,768]{2,1,0:T(8,128)(2,1)}, u32[]{:S(2)}, u32[]{:S(2)}) collective-permute-start(bf16[1,1536,768]{2,1,0:T(8,128)(2,1)} %up_hbm.3), channel_id=1, source_target_pairs={{0,1},{1,0},{2,3},{3,2},{4,5},{5,4},{6,7},{7,6},{8,9},{9,8},{10,11... | collective-permute-start | bytes 7077896 | tf_op jit(solution)/shard_map/ppermute | solution.py:33
  12.1 33.6 %collective-permute-start.7 = (bf16[1,768,1536]{2,1,0:T(8,128)(2,1)}, bf16[1,768,1536]{2,1,0:T(8,128)(2,1)}, u32[]{:S(2)}, u32[]{:S(2)}) collective-permute-start(bf16[1,768,1536]{2,1,0:T(8,128)(2,1)} %down_hbm.3), channel_id=1, source_target_pairs={{0,1},{1,0},{2,3},{3,2},{4,5},{5,4},{6,7},{7,6},{8,9},{9,8},{10,11... | collective-permute-start | bytes 7077896 | tf_op jit(solution)/shard_map/ppermute | solution.py:33
  12.6 15.1 %collective-permute-start.2 = (bf16[64,1536]{1,0:T(8,128)(2,1)S(1)}, bf16[64,1536]{1,0:T(8,128)(2,1)S(1)}, u32[]{:S(2)}, u32[]{:S(2)}) collective-permute-start(bf16[64,1536]{1,0:T(8,128)(2,1)S(1)} %get-tuple-element.39), channel_id=1, source_target_pairs={{0,16},{2,18},{4,20},{6,22},{8,24},{10,26},{12,28},{14,30},{16,0},... | collective-permute-start | bytes 589832 | tf_op jit(solution)/shard_map/ppermute | solution.py:38
  18.0 9.8 %collective-permute-start.3 = (f32[8,128]{1,0:T(8,128)S(1)}, f32[8,128]{1,0:T(8,128)S(1)}, u32[]{:S(2)}, u32[]{:S(2)}) collective-permute-start(f32[8,128]{1,0:T(8,128)S(1)} %pad_maximum_fusion.1.notes_ref.weights_ref), channel_id=1, source_target_pairs={{0,16},{2,18},{4,20},{6,22},{8,24},{10,26},{12,28},{14,30},{16,0},... | collective-permute-start | bytes 12296 | tf_op jit(solution)/shard_map/ppermute | solution.py:38
  27.8 1.4 %collective-permute-start.4 = (bf16[64,1536]{1,0:T(8,128)(2,1)S(1)}, bf16[64,1536]{1,0:T(8,128)(2,1)S(1)}, u32[]{:S(2)}, u32[]{:S(2)}) collective-permute-start(bf16[64,1536]{1,0:T(8,128)(2,1)S(1)} %collective-permute-done.2.refs_0_), channel_id=1, source_target_pairs={{0,1},{1,0},{2,3},{3,2},{4,5},{5,4},{6,7},{7,6},{8,9},{9,8},{10,11... | collective-permute-start | bytes 589832 | tf_op jit(solution)/shard_map/ppermute | solution.py:33
  45.7 14.5 %all-to-all-start.1 = ((bf16[8,32,1536]{2,1,0:T(8,128)(2,1)}), bf16[8,32,1536]{2,1,0:T(8,128)(2,1)S(1)}, u32[]{:S(2)}, u32[]{:S(2)}) async-start(bf16[8,32,1536]{2,1,0:T(8,128)(2,1)} %bitcast.7), calls=%async_computation.1 | async-start | bytes 1572864 | tf_op jit(solution)/shard_map/all_to_all | solution.py:403
  60.2 3.6 %copy-start.1 = (bf16[8,32,1536]{2,1,0:T(8,128)(2,1)}, bf16[8,32,1536]{2,1,0:T(8,128)(2,1)S(1)}, u32[]{:S(2)}) copy-start(bf16[8,32,1536]{2,1,0:T(8,128)(2,1)S(1)} %all-to-all-done.1) | copy-start | bytes 2359300
  60.2 14.6 %all-to-all-start.2 = ((bf16[8,32,1536]{2,1,0:T(8,128)(2,1)}), bf16[8,32,1536]{2,1,0:T(8,128)(2,1)S(1)}, u32[]{:S(2)}, u32[]{:S(2)}) async-start(bf16[8,32,1536]{2,1,0:T(8,128)(2,1)} %bitcast.20), calls=%async_computation.2 | async-start | bytes 1572864 | tf_op jit(solution)/shard_map/all_to_all | solution.py:403
  74.8 18.8 %all-to-all-start.3 = ((bf16[8,32,1536]{2,1,0:T(8,128)(2,1)}), bf16[8,32,1536]{2,1,0:T(8,128)(2,1)S(1)}, u32[]{:S(2)}, u32[]{:S(2)}) async-start(bf16[8,32,1536]{2,1,0:T(8,128)(2,1)} %bitcast.17), calls=%async_computation.3 | async-start | bytes 1572864 | tf_op jit(solution)/shard_map/all_to_all | solution.py:403
  78.8 1.5 %collective-permute-start.8 = (bf16[128,768]{1,0:T(8,128)(2,1)S(1)}, bf16[128,768]{1,0:T(8,128)(2,1)S(1)}, u32[]{:S(2)}, u32[]{:S(2)}) collective-permute-start(bf16[128,768]{1,0:T(8,128)(2,1)S(1)} %get-tuple-element.60), channel_id=1, source_target_pairs={{0,1},{1,0},{2,3},{3,2},{4,5},{5,4},{6,7},{7,6},{8,9},{9,8},{10,11... | collective-permute-start | bytes 589832 | tf_op jit(solution)/shard_map/ppermute | solution.py:33
  80.4 13.7 %collective-permute-start.9 = (bf16[128,768]{1,0:T(8,128)(2,1)S(1)}, bf16[128,768]{1,0:T(8,128)(2,1)S(1)}, u32[]{:S(2)}, u32[]{:S(2)}) collective-permute-start(bf16[128,768]{1,0:T(8,128)(2,1)S(1)} %add_convert_fusion.1), channel_id=1, source_target_pairs={{0,16},{2,18},{4,20},{6,22},{8,24},{10,26},{12,28},{14,30},{16,0},... | collective-permute-start | bytes 589832 | tf_op jit(solution)/shard_map/ppermute | solution.py:38
  94.1 1.5 %collective-permute-start.10 = (bf16[128,768]{1,0:T(8,128)(2,1)S(1)}, bf16[128,768]{1,0:T(8,128)(2,1)S(1)}, u32[]{:S(2)}, u32[]{:S(2)}) collective-permute-start(bf16[128,768]{1,0:T(8,128)(2,1)S(1)} %get-tuple-element.61), channel_id=1, source_target_pairs={{0,1},{1,0},{2,3},{3,2},{4,5},{5,4},{6,7},{7,6},{8,9},{9,8},{10,11... | collective-permute-start | bytes 589832 | tf_op jit(solution)/shard_map/ppermute | solution.py:33

commit v2 on v1

--- a/solution.py
+++ b/solution.py
@@ -69,7 +69,7 @@
     first_ref, sink_ref, q_ref, kv_ref, before_ref, w_hbm, out_ref, w_ref, att_ref, sum_ref, sems
 ):
     tokens, width = q_ref.shape
-    kv_heads = kv_ref.shape[1] // (2 * HEAD_SIZE)
+    kv_heads = kv_ref.shape[1] // HEAD_SIZE
     pairs = width // LANES // kv_heads
     depth = pairs * LANES
     spans = [pl.ds(head * depth, depth) for head in range(kv_heads)]
@@ -93,12 +93,12 @@
     before_factor = jnp.where(own, 0.0, usable).astype(jnp.bfloat16)
     head_lanes = jnp.where(low, 1.0, 0.0).astype(jnp.bfloat16), jnp.where(low, 0.0, 1.0).astype(jnp.bfloat16)
     ones = jnp.concatenate(head_lanes * 2, axis=0)
-    keys_before = [jnp.concatenate(doubled(before_ref[:, :LANES], head), axis=0) for head in range(kv_heads)]
-    values_before = [doubled(before_ref[:, LANES:], head) for head in range(kv_heads)]
+    keys_before = [jnp.concatenate(doubled(before_ref[:tokens, :], head), axis=0) for head in range(kv_heads)]
+    values_before = [doubled(before_ref[tokens:, :], head) for head in range(kv_heads)]
     contract = (((1,), (1,)), ((), ()))
     for head in range(kv_heads):
-        keys = jnp.concatenate(doubled(kv_ref[:, :LANES], head), axis=0)
-        values = jnp.concatenate(doubled(kv_ref[:, LANES:], head) + values_before[head], axis=0)
+        keys = jnp.concatenate(doubled(kv_ref[:tokens, :], head), axis=0)
+        values = jnp.concatenate(doubled(kv_ref[tokens:, :], head) + values_before[head], axis=0)
         values = jnp.concatenate([values, ones], axis=1)
         for j in range(head * pairs, (head + 1) * pairs):
             q = q_ref[:, j * LANES : (j + 1) * LANES]
@@ -143,7 +143,7 @@
             pltpu.VMEM(w_out.shape, jnp.bfloat16),
             pltpu.VMEM(q.shape, jnp.bfloat16),
             pltpu.VMEM((tokens, w_out.shape[1]), jnp.float32),
-            pltpu.SemaphoreType.DMA((key_values.shape[1] // (2 * HEAD_SIZE),)),
+            pltpu.SemaphoreType.DMA((key_values.shape[1] // HEAD_SIZE,)),
         ],
         compiler_params=pltpu.CompilerParams(vmem_limit_bytes=54_000_000),
         cost_estimate=cost(2 * tokens * w_out.size * 2, 2 * w_out.size, tokens * tokens * q.shape[1] // HEAD_SIZE),
@@ -383,7 +383,7 @@
     base = jnp.where(at_seq < group, 0, experts // 2).astype(jnp.int32).reshape(1)
     side = lax.axis_index("tp").astype(jnp.int32).reshape(1)
     first = (at_seq == 0).astype(jnp.int32).reshape(1)
-    key_values = lax.optimization_barrier(jnp.concatenate([rotated_key_rows, value_row_matrix], axis=1))
+    key_values = lax.optimization_barrier(jnp.concatenate([rotated_key_rows, value_row_matrix], axis=0))
     before = passed_along(key_values, "seq", 1)
     sinks = jnp.broadcast_to(learned_sink_scores[:, None], (learned_sink_scores.shape[0], LANES))
     sinks, queries = lax.optimization_barrier((sinks, query_rows))

time: 96.9 us -> 96.9 us (level)
  no operation moved by 1% of the time
where the time goes in v2:
time: 96.9 us; the launch traced here: 96.3 us
  waiting for transfers between devices  30.3 us (31%)
  starting transfers between devices  23.5 us (24%)
  Pallas kernels  23.1 us (24%)
  blocking collectives  15.9 us (16%)
  other arithmetic  2.61 us (3%)
    pallas_call x2, Pallas kernels, expert_layer(): pl.pallas_call(expert_kernel, out_shape=shape_of((rows, width)), in_specs...  17 us
    all_to_all x3, waiting for transfers between devices, exchanged(): lax.all_to_all(block, 'seq', split_axis=0, concat_axis=0, axis_index_grou...  16.5 us
    all_to_all x1, blocking collectives, exchanged(): lax.all_to_all(block, 'seq', split_axis=0, concat_axis=0, axis_index_grou...  15.9 us
    all_to_all x3, starting transfers between devices, exchanged(): lax.all_to_all(block, 'seq', split_axis=0, concat_axis=0, axis_index_grou...  10.7 us
    ppermute x3, waiting for transfers between devices, swapped_halves(): lax.ppermute(block, axis, [(i, (i + count // 2) % count) for i in range(c...  8.22 us
    ppermute x3, starting transfers between devices, swapped_halves(): lax.ppermute(block, axis, [(i, (i + count // 2) % count) for i in range(c...  7.1 us
    ppermute x7, waiting for transfers between devices, swapped(): return lax.ppermute(block, axis, [(i, count - 1 - i) for i in range(count)])  5.44 us
    ppermute x1, starting transfers between devices, passed_along(): return lax.ppermute(block, axis, route)  4.83 us
  transfers between devices with their start and end apart: 14, of which 9 were waited for; matrix products, arithmetic and copies ran while one was open for 2% of the time, Pallas kernels for 21%

profile of v2, /device:TPU:0, one launch (start us, length us, event | category | flops | bytes accessed | tf_op | source)
XLA Modules:
  0.0 96.3 jit_solution(13943024039135511663)
XLA Ops:
  0.0 0.8 pad_maximum_fusion.kv_ref
  0.8 4.8 %collective-permute-start = (bf16[256,128]{1,0:T(8,128)(2,1)S(1)}, bf16[256,128]{1,0:T(8,128)(2,1)S(1)}, u32[]{:S(2)}, u32[]{:S(2)}) collective-permute-start(bf16[256,128]{1,0:T(8,128)(2,1)S(1)} %pad_maximum_fusion.kv_ref), channel_id=1, source_target_pairs={{0,2},{2,4},{4,6},{6,8},{8,10},{10,12},{12,14},{14,16},{16,18},{18... | collective-permute-start | bytes 196616 | tf_op jit(solution)/shard_map/ppermute | solution.py:28
  5.7 0.7 broadcast_in_dim.2.sink_ref
  6.4 1.0 %broadcast_multiply_fusion.q_ref = bf16[128,1024]{1,0:T(8,128)(2,1)S(1)} fusion(bf16[128,1024]{1,0:T(8,128)(2,1)} %param.13), kind=kLoop, calls=%fused_computation.2 | loop fusion | flops 131072 | bytes 524288 | tf_op jit(solution)/shard_map/mul | solution.py:390
  7.4 0.2 collective-permute-done.before_ref
  7.6 2.7 %attention.1.near_ref = bf16[128,1536]{1,0:T(8,128)(2,1)S(1)} custom-call(s32[1]{0:T(128)} %bitcast.4.first_ref, f32[16,128]{1,0:T(8,128)S(1)} %broadcast_in_dim.2.sink_ref, bf16[128,1024]{1,0:T(8,128)(2,1)S(1)} %broadcast_multiply_fusion.q_ref, bf16[256,128]{1,0:T(8,128)(2,1)S(1)} %pad_maximum_fusion.kv_ref, ...), custom_call_target="tpu_custom_call" | custom-call | flops 805306368 | bytes 3145728 | tf_op jit(solution)/shard_map/attention/pallas_call | solution.py:137
  10.4 0.5 collective-permute-start.5
  10.9 0.1 collective-permute-start.6
  11.0 1.1 %collective-permute-done.1.far_ref = bf16[128,1536]{1,0:T(8,128)(2,1)S(1)} collective-permute-done((bf16[128,1536]{1,0:T(8,128)(2,1)S(1)}, bf16[128,1536]{1,0:T(8,128)(2,1)S(1)}, u32[]{:S(2)}, u32[]{:S(2)}) %collective-permute-start.1) | collective-permute-done | bytes 393248 | tf_op jit(solution)/shard_map/ppermute | solution.py:33
  12.1 0.1 collective-permute-start.7
  12.2 0.4 norm.1
  12.6 5.3 %collective-permute-start.2 = (bf16[64,1536]{1,0:T(8,128)(2,1)S(1)}, bf16[64,1536]{1,0:T(8,128)(2,1)S(1)}, u32[]{:S(2)}, u32[]{:S(2)}) collective-permute-start(bf16[64,1536]{1,0:T(8,128)(2,1)S(1)} %get-tuple-element.39), channel_id=1, source_target_pairs={{0,16},{2,18},{4,20},{6,22},{8,24},{10,26},{12,28},{14,30},{16,0},... | collective-permute-start | bytes 589832 | tf_op jit(solution)/shard_map/ppermute | solution.py:38
  18.0 0.1 collective-permute-start.3
  18.1 1.5 %packed_rows.2 = (bf16[256,1536]{1,0:T(8,128)(2,1)}, s32[4,128]{1,0:T(4,128)S(1)}) custom-call(s32[1]{0:T(128)} %bitcast.1.base_ref, s32[1]{0:T(128)} %bitcast.side_ref, f32[8,128]{1,0:T(8,128)S(1)} %pad_maximum_fusion.1.notes_ref.weights_ref, bf16[128,1536]{1,0:T(8,128)(2,1)S(1)} %get-tuple-element.37.refs_0_), custom_call_target="tpu_custom_call" | custom-call | flops 100663296 | bytes 786432 | tf_op jit(solution)/shard_map/packed_rows/pallas_call | solution.py:209
  19.6 8.2 %collective-permute-done.3.notes_ref.weights_ref = f32[8,128]{1,0:T(8,128)S(1)} collective-permute-done((f32[8,128]{1,0:T(8,128)S(1)}, f32[8,128]{1,0:T(8,128)S(1)}, u32[]{:S(2)}, u32[]{:S(2)}) %collective-permute-start.3) | collective-permute-done | bytes 4128 | tf_op jit(solution)/shard_map/ppermute | solution.py:38
  27.8 1.4 %collective-permute-done.4.refs_1_ = bf16[64,1536]{1,0:T(8,128)(2,1)S(1)} collective-permute-done((bf16[64,1536]{1,0:T(8,128)(2,1)S(1)}, bf16[64,1536]{1,0:T(8,128)(2,1)S(1)}, u32[]{:S(2)}, u32[]{:S(2)}) %collective-permute-start.4) | collective-permute-done | bytes 196640 | tf_op jit(solution)/shard_map/ppermute | solution.py:33
  29.2 0.5 packed_rows.3
  29.7 15.9 %all_to_all.20 = bf16[8,32,1536]{2,1,0:T(8,128)(2,1)} all-to-all(bf16[8,32,1536]{2,1,0:T(8,128)(2,1)S(1)} %bitcast.16), channel_id=1, replica_groups={{0,2,4,6,8,10,12,14},{16,18,20,22,24,26,28,30},{1,3,5,7,9,11,13,15},{17..., dimensions={0} | all-to-all | bytes 1572864 | tf_op jit(solution)/shard_map/all_to_all | solution.py:403
  45.7 3.6 %all-to-all-start.1 = ((bf16[8,32,1536]{2,1,0:T(8,128)(2,1)}), bf16[8,32,1536]{2,1,0:T(8,128)(2,1)S(1)}, u32[]{:S(2)}, u32[]{:S(2)}) async-start(bf16[8,32,1536]{2,1,0:T(8,128)(2,1)} %bitcast.7), calls=%async_computation.1 | async-start | bytes 1572864 | tf_op jit(solution)/shard_map/all_to_all | solution.py:403
  49.2 8.5 %expert_layer.2 = bf16[256,1536]{1,0:T(8,128)(2,1)} custom-call(bf16[256,1536]{1,0:T(8,128)(2,1)} %bitcast.19, bf16[1,1536,768]{2,1,0:T(8,128)(2,1)} %gate_hbm.3, bf16[1,1536,768]{2,1,0:T(8,128)(2,1)} %up_hbm.3, bf16[1,768,1536]{2,1,0:T(8,128)(2,1)} %down_hbm.3, bf16[1,1536,768]{2,1,0:T(8,128)(2,1)} %collective-permute-done.5.gate_too_hbm, ...), custom_call_target="tpu_custom_call" | custom-call | flops 3623878656 | bytes 14155776 | tf_op jit(solution)/shard_map/expert_layer/pallas_call | solution.py:295
  57.7 2.5 %all-to-all-done.1 = bf16[8,32,1536]{2,1,0:T(8,128)(2,1)S(1)} async-done(((bf16[8,32,1536]{2,1,0:T(8,128)(2,1)}), bf16[8,32,1536]{2,1,0:T(8,128)(2,1)S(1)}, u32[]{:S(2)}, u32[]{:S(2)}) %all-to-all-start.1) | async-done | bytes 786464 | tf_op jit(solution)/shard_map/all_to_all | solution.py:403
  60.2 3.5 %all-to-all-start.2 = ((bf16[8,32,1536]{2,1,0:T(8,128)(2,1)}), bf16[8,32,1536]{2,1,0:T(8,128)(2,1)S(1)}, u32[]{:S(2)}, u32[]{:S(2)}) async-start(bf16[8,32,1536]{2,1,0:T(8,128)(2,1)} %bitcast.20), calls=%async_computation.2 | async-start | bytes 1572864 | tf_op jit(solution)/shard_map/all_to_all | solution.py:403
  63.8 8.5 %expert_layer.3 = bf16[256,1536]{1,0:T(8,128)(2,1)} custom-call(bf16[256,1536]{1,0:T(8,128)(2,1)} %bitcast.18, bf16[1,1536,768]{2,1,0:T(8,128)(2,1)} %gate_hbm.3, bf16[1,1536,768]{2,1,0:T(8,128)(2,1)} %up_hbm.3, bf16[1,768,1536]{2,1,0:T(8,128)(2,1)} %down_hbm.3, bf16[1,1536,768]{2,1,0:T(8,128)(2,1)} %collective-permute-done.5.gate_too_hbm, ...), custom_call_target="tpu_custom_call" | custom-call | flops 3623878656 | bytes 14155776 | tf_op jit(solution)/shard_map/expert_layer/pallas_call | solution.py:295
  72.3 2.5 %all-to-all-done.2 = bf16[8,32,1536]{2,1,0:T(8,128)(2,1)S(1)} async-done(((bf16[8,32,1536]{2,1,0:T(8,128)(2,1)}), bf16[8,32,1536]{2,1,0:T(8,128)(2,1)S(1)}, u32[]{:S(2)}, u32[]{:S(2)}) %all-to-all-start.2) | async-done | bytes 786464 | tf_op jit(solution)/shard_map/all_to_all | solution.py:403
  74.8 3.5 %all-to-all-start.3 = ((bf16[8,32,1536]{2,1,0:T(8,128)(2,1)}), bf16[8,32,1536]{2,1,0:T(8,128)(2,1)S(1)}, u32[]{:S(2)}, u32[]{:S(2)}) async-start(bf16[8,32,1536]{2,1,0:T(8,128)(2,1)} %bitcast.17), calls=%async_computation.3 | async-start | bytes 1572864 | tf_op jit(solution)/shard_map/all_to_all | solution.py:403
  78.3 0.5 combine.3
  78.9 1.4 %collective-permute-done.8 = bf16[128,768]{1,0:T(8,128)(2,1)S(1)} collective-permute-done((bf16[128,768]{1,0:T(8,128)(2,1)S(1)}, bf16[128,768]{1,0:T(8,128)(2,1)S(1)}, u32[]{:S(2)}, u32[]{:S(2)}) %collective-permute-start.8) | collective-permute-done | bytes 196640 | tf_op jit(solution)/shard_map/ppermute | solution.py:33
  80.4 1.7 %collective-permute-start.9 = (bf16[128,768]{1,0:T(8,128)(2,1)S(1)}, bf16[128,768]{1,0:T(8,128)(2,1)S(1)}, u32[]{:S(2)}, u32[]{:S(2)}) collective-permute-start(bf16[128,768]{1,0:T(8,128)(2,1)S(1)} %add_convert_fusion.1), channel_id=1, source_target_pairs={{0,16},{2,18},{4,20},{6,22},{8,24},{10,26},{12,28},{14,30},{16,0},... | collective-permute-start | bytes 589832 | tf_op jit(solution)/shard_map/ppermute | solution.py:38
  82.0 11.5 %all-to-all-done.3 = bf16[8,32,1536]{2,1,0:T(8,128)(2,1)S(1)} async-done(((bf16[8,32,1536]{2,1,0:T(8,128)(2,1)}), bf16[8,32,1536]{2,1,0:T(8,128)(2,1)S(1)}, u32[]{:S(2)}, u32[]{:S(2)}) %all-to-all-start.3) | async-done | bytes 786464 | tf_op jit(solution)/shard_map/all_to_all | solution.py:403
  93.6 0.5 combine.2
  94.1 1.4 %collective-permute-done.10 = bf16[128,768]{1,0:T(8,128)(2,1)S(1)} collective-permute-done((bf16[128,768]{1,0:T(8,128)(2,1)S(1)}, bf16[128,768]{1,0:T(8,128)(2,1)S(1)}, u32[]{:S(2)}, u32[]{:S(2)}) %collective-permute-start.10) | collective-permute-done | bytes 196640 | tf_op jit(solution)/shard_map/ppermute | solution.py:33
  95.6 0.7 add_convert_fusion
  (23 shorter events, 0.3 us)
Async XLA Ops:
  0.0 12.2 %copy-start.2 = (f32[1536]{0:T(1024)S(1)}, f32[1536]{0:T(1024)}, u32[]{:S(2)}) copy-start(f32[1536]{0:T(1024)} %param.18) | copy-start | bytes 18436
  0.0 12.2 %copy-start = (bf16[128,1536]{1,0:T(8,128)(2,1)S(1)}, bf16[128,1536]{1,0:T(8,128)(2,1)}, u32[]{:S(2)}) copy-start(bf16[128,1536]{1,0:T(8,128)(2,1)} %residual_ref.1) | copy-start | bytes 1179652
  0.8 6.7 %collective-permute-start = (bf16[256,128]{1,0:T(8,128)(2,1)S(1)}, bf16[256,128]{1,0:T(8,128)(2,1)S(1)}, u32[]{:S(2)}, u32[]{:S(2)}) collective-permute-start(bf16[256,128]{1,0:T(8,128)(2,1)S(1)} %pad_maximum_fusion.kv_ref), channel_id=1, source_target_pairs={{0,2},{2,4},{4,6},{6,8},{8,10},{10,12},{12,14},{14,16},{16,18},{18... | collective-permute-start | bytes 196616 | tf_op jit(solution)/shard_map/ppermute | solution.py:28
  7.6 10.4 %copy-start.3 = (s32[128,4]{0,1:T(4,128)S(1)}, s32[128,4]{0,1:T(4,128)}, u32[]{:S(2)}) copy-start(s32[128,4]{0,1:T(4,128)} %param.19) | copy-start | bytes 6148
  7.6 10.4 %copy-start.4 = (f32[128,4]{0,1:T(4,128)S(1)}, f32[128,4]{0,1:T(4,128)}, u32[]{:S(2)}) copy-start(f32[128,4]{0,1:T(4,128)} %param.20) | copy-start | bytes 6148
  10.3 1.8 %collective-permute-start.1 = (bf16[128,1536]{1,0:T(8,128)(2,1)S(1)}, bf16[128,1536]{1,0:T(8,128)(2,1)S(1)}, u32[]{:S(2)}, u32[]{:S(2)}) collective-permute-start(bf16[128,1536]{1,0:T(8,128)(2,1)S(1)} %attention.1.near_ref), channel_id=1, source_target_pairs={{0,1},{1,0},{2,3},{3,2},{4,5},{5,4},{6,7},{7,6},{8,9},{9,8},{10,11... | collective-permute-start | bytes 1179656 | tf_op jit(solution)/shard_map/ppermute | solution.py:33
  10.4 35.3 %collective-permute-start.5 = (bf16[1,1536,768]{2,1,0:T(8,128)(2,1)}, bf16[1,1536,768]{2,1,0:T(8,128)(2,1)}, u32[]{:S(2)}, u32[]{:S(2)}) collective-permute-start(bf16[1,1536,768]{2,1,0:T(8,128)(2,1)} %gate_hbm.3), channel_id=1, source_target_pairs={{0,1},{1,0},{2,3},{3,2},{4,5},{5,4},{6,7},{7,6},{8,9},{9,8},{10,11... | collective-permute-start | bytes 7077896 | tf_op jit(solution)/shard_map/ppermute | solution.py:33
  10.9 34.8 %collective-permute-start.6 = (bf16[1,1536,768]{2,1,0:T(8,128)(2,1)}, bf16[1,1536,768]{2,1,0:T(8,128)(2,1)}, u32[]{:S(2)}, u32[]{:S(2)}) collective-permute-start(bf16[1,1536,768]{2,1,0:T(8,128)(2,1)} %up_hbm.3), channel_id=1, source_target_pairs={{0,1},{1,0},{2,3},{3,2},{4,5},{5,4},{6,7},{7,6},{8,9},{9,8},{10,11... | collective-permute-start | bytes 7077896 | tf_op jit(solution)/shard_map/ppermute | solution.py:33
  12.1 33.6 %collective-permute-start.7 = (bf16[1,768,1536]{2,1,0:T(8,128)(2,1)}, bf16[1,768,1536]{2,1,0:T(8,128)(2,1)}, u32[]{:S(2)}, u32[]{:S(2)}) collective-permute-start(bf16[1,768,1536]{2,1,0:T(8,128)(2,1)} %down_hbm.3), channel_id=1, source_target_pairs={{0,1},{1,0},{2,3},{3,2},{4,5},{5,4},{6,7},{7,6},{8,9},{9,8},{10,11... | collective-permute-start | bytes 7077896 | tf_op jit(solution)/shard_map/ppermute | solution.py:33
  12.6 15.2 %collective-permute-start.2 = (bf16[64,1536]{1,0:T(8,128)(2,1)S(1)}, bf16[64,1536]{1,0:T(8,128)(2,1)S(1)}, u32[]{:S(2)}, u32[]{:S(2)}) collective-permute-start(bf16[64,1536]{1,0:T(8,128)(2,1)S(1)} %get-tuple-element.39), channel_id=1, source_target_pairs={{0,16},{2,18},{4,20},{6,22},{8,24},{10,26},{12,28},{14,30},{16,0},... | collective-permute-start | bytes 589832 | tf_op jit(solution)/shard_map/ppermute | solution.py:38
  18.0 9.8 %collective-permute-start.3 = (f32[8,128]{1,0:T(8,128)S(1)}, f32[8,128]{1,0:T(8,128)S(1)}, u32[]{:S(2)}, u32[]{:S(2)}) collective-permute-start(f32[8,128]{1,0:T(8,128)S(1)} %pad_maximum_fusion.1.notes_ref.weights_ref), channel_id=1, source_target_pairs={{0,16},{2,18},{4,20},{6,22},{8,24},{10,26},{12,28},{14,30},{16,0},... | collective-permute-start | bytes 12296 | tf_op jit(solution)/shard_map/ppermute | solution.py:38
  27.8 1.4 %collective-permute-start.4 = (bf16[64,1536]{1,0:T(8,128)(2,1)S(1)}, bf16[64,1536]{1,0:T(8,128)(2,1)S(1)}, u32[]{:S(2)}, u32[]{:S(2)}) collective-permute-start(bf16[64,1536]{1,0:T(8,128)(2,1)S(1)} %collective-permute-done.2.refs_0_), channel_id=1, source_target_pairs={{0,1},{1,0},{2,3},{3,2},{4,5},{5,4},{6,7},{7,6},{8,9},{9,8},{10,11... | collective-permute-start | bytes 589832 | tf_op jit(solution)/shard_map/ppermute | solution.py:33
  45.7 14.5 %all-to-all-start.1 = ((bf16[8,32,1536]{2,1,0:T(8,128)(2,1)}), bf16[8,32,1536]{2,1,0:T(8,128)(2,1)S(1)}, u32[]{:S(2)}, u32[]{:S(2)}) async-start(bf16[8,32,1536]{2,1,0:T(8,128)(2,1)} %bitcast.7), calls=%async_computation.1 | async-start | bytes 1572864 | tf_op jit(solution)/shard_map/all_to_all | solution.py:403
  60.2 3.6 %copy-start.1 = (bf16[8,32,1536]{2,1,0:T(8,128)(2,1)}, bf16[8,32,1536]{2,1,0:T(8,128)(2,1)S(1)}, u32[]{:S(2)}) copy-start(bf16[8,32,1536]{2,1,0:T(8,128)(2,1)S(1)} %all-to-all-done.1) | copy-start | bytes 2359300
  60.2 14.6 %all-to-all-start.2 = ((bf16[8,32,1536]{2,1,0:T(8,128)(2,1)}), bf16[8,32,1536]{2,1,0:T(8,128)(2,1)S(1)}, u32[]{:S(2)}, u32[]{:S(2)}) async-start(bf16[8,32,1536]{2,1,0:T(8,128)(2,1)} %bitcast.20), calls=%async_computation.2 | async-start | bytes 1572864 | tf_op jit(solution)/shard_map/all_to_all | solution.py:403
  74.8 18.8 %all-to-all-start.3 = ((bf16[8,32,1536]{2,1,0:T(8,128)(2,1)}), bf16[8,32,1536]{2,1,0:T(8,128)(2,1)S(1)}, u32[]{:S(2)}, u32[]{:S(2)}) async-start(bf16[8,32,1536]{2,1,0:T(8,128)(2,1)} %bitcast.17), calls=%async_computation.3 | async-start | bytes 1572864 | tf_op jit(solution)/shard_map/all_to_all | solution.py:403
  78.8 1.5 %collective-permute-start.8 = (bf16[128,768]{1,0:T(8,128)(2,1)S(1)}, bf16[128,768]{1,0:T(8,128)(2,1)S(1)}, u32[]{:S(2)}, u32[]{:S(2)}) collective-permute-start(bf16[128,768]{1,0:T(8,128)(2,1)S(1)} %get-tuple-element.60), channel_id=1, source_target_pairs={{0,1},{1,0},{2,3},{3,2},{4,5},{5,4},{6,7},{7,6},{8,9},{9,8},{10,11... | collective-permute-start | bytes 589832 | tf_op jit(solution)/shard_map/ppermute | solution.py:33
  80.4 13.7 %collective-permute-start.9 = (bf16[128,768]{1,0:T(8,128)(2,1)S(1)}, bf16[128,768]{1,0:T(8,128)(2,1)S(1)}, u32[]{:S(2)}, u32[]{:S(2)}) collective-permute-start(bf16[128,768]{1,0:T(8,128)(2,1)S(1)} %add_convert_fusion.1), channel_id=1, source_target_pairs={{0,16},{2,18},{4,20},{6,22},{8,24},{10,26},{12,28},{14,30},{16,0},... | collective-permute-start | bytes 589832 | tf_op jit(solution)/shard_map/ppermute | solution.py:38
  94.1 1.5 %collective-permute-start.10 = (bf16[128,768]{1,0:T(8,128)(2,1)S(1)}, bf16[128,768]{1,0:T(8,128)(2,1)S(1)}, u32[]{:S(2)}, u32[]{:S(2)}) collective-permute-start(bf16[128,768]{1,0:T(8,128)(2,1)S(1)} %get-tuple-element.61), channel_id=1, source_target_pairs={{0,1},{1,0},{2,3},{3,2},{4,5},{5,4},{6,7},{7,6},{8,9},{9,8},{10,11... | collective-permute-start | bytes 589832 | tf_op jit(solution)/shard_map/ppermute | solution.py:33

commit v3 on v1

--- a/solution.py
+++ b/solution.py
@@ -97,13 +97,13 @@
     values_before = [doubled(before_ref[:, LANES:], head) for head in range(kv_heads)]
     contract = (((1,), (1,)), ((), ()))
     for head in range(kv_heads):
-        keys = jnp.concatenate(doubled(kv_ref[:, :LANES], head), axis=0)
+        keys = jnp.concatenate(doubled(kv_ref[:, :LANES], head) + [keys_before[head]], axis=0)
         values = jnp.concatenate(doubled(kv_ref[:, LANES:], head) + values_before[head], axis=0)
         values = jnp.concatenate([values, ones], axis=1)
         for j in range(head * pairs, (head + 1) * pairs):
             q = q_ref[:, j * LANES : (j + 1) * LANES]
-            near = lax.dot_general(q, keys, contract, preferred_element_type=jnp.float32)
-            far = lax.dot_general(q, keys_before[head], contract, preferred_element_type=jnp.float32)
+            scores = lax.dot_general(q, keys, contract, preferred_element_type=jnp.float32)
+            near, far = scores[:, : 2 * tokens], scores[:, 2 * tokens :]
             terms, sinks = [], []
             for at in range(2):
                 span = slice(at * tokens, (at + 1) * tokens)

time: 96.9 us -> 96.9 us (level)
  no operation moved by 1% of the time
where the time goes in v3:
time: 96.9 us; the launch traced here: 96.3 us
  waiting for transfers between devices  30.3 us (31%)
  starting transfers between devices  23.5 us (24%)
  Pallas kernels  23.1 us (24%)
  blocking collectives  15.9 us (16%)
  other arithmetic  2.61 us (3%)
    pallas_call x2, Pallas kernels, expert_layer(): pl.pallas_call(expert_kernel, out_shape=shape_of((rows, width)), in_specs...  17 us
    all_to_all x3, waiting for transfers between devices, exchanged(): lax.all_to_all(block, 'seq', split_axis=0, concat_axis=0, axis_index_grou...  16.5 us
    all_to_all x1, blocking collectives, exchanged(): lax.all_to_all(block, 'seq', split_axis=0, concat_axis=0, axis_index_grou...  15.9 us
    all_to_all x3, starting transfers between devices, exchanged(): lax.all_to_all(block, 'seq', split_axis=0, concat_axis=0, axis_index_grou...  10.7 us
    ppermute x3, waiting for transfers between devices, swapped_halves(): lax.ppermute(block, axis, [(i, (i + count // 2) % count) for i in range(c...  8.22 us
    ppermute x3, starting transfers between devices, swapped_halves(): lax.ppermute(block, axis, [(i, (i + count // 2) % count) for i in range(c...  7.1 us
    ppermute x7, waiting for transfers between devices, swapped(): return lax.ppermute(block, axis, [(i, count - 1 - i) for i in range(count)])  5.44 us
    ppermute x1, starting transfers between devices, passed_along(): return lax.ppermute(block, axis, route)  4.84 us
  transfers between devices with their start and end apart: 14, of which 9 were waited for; matrix products, arithmetic and copies ran while one was open for 2% of the time, Pallas kernels for 21%

profile of v3, /device:TPU:0, one launch (start us, length us, event | category | flops | bytes accessed | tf_op | source)
XLA Modules:
  0.0 96.3 jit_solution(921956455192887418)
XLA Ops:
  0.0 0.8 pad_maximum_fusion.kv_ref
  0.8 4.8 %collective-permute-start = (bf16[128,256]{1,0:T(8,128)(2,1)S(1)}, bf16[128,256]{1,0:T(8,128)(2,1)S(1)}, u32[]{:S(2)}, u32[]{:S(2)}) collective-permute-start(bf16[128,256]{1,0:T(8,128)(2,1)S(1)} %pad_maximum_fusion.kv_ref), channel_id=1, source_target_pairs={{0,2},{2,4},{4,6},{6,8},{8,10},{10,12},{12,14},{14,16},{16,18},{18... | collective-permute-start | bytes 196616 | tf_op jit(solution)/shard_map/ppermute | solution.py:28
  5.7 0.7 broadcast_in_dim.2.sink_ref
  6.4 1.0 %broadcast_multiply_fusion.q_ref = bf16[128,1024]{1,0:T(8,128)(2,1)S(1)} fusion(bf16[128,1024]{1,0:T(8,128)(2,1)} %param.13), kind=kLoop, calls=%fused_computation.2 | loop fusion | flops 131072 | bytes 524288 | tf_op jit(solution)/shard_map/mul | solution.py:390
  7.4 0.2 collective-permute-done.before_ref
  7.6 2.7 %attention.1.near_ref = bf16[128,1536]{1,0:T(8,128)(2,1)S(1)} custom-call(s32[1]{0:T(128)} %bitcast.4.first_ref, f32[16,128]{1,0:T(8,128)S(1)} %broadcast_in_dim.2.sink_ref, bf16[128,1024]{1,0:T(8,128)(2,1)S(1)} %broadcast_multiply_fusion.q_ref, bf16[128,256]{1,0:T(8,128)(2,1)S(1)} %pad_maximum_fusion.kv_ref, ...), custom_call_target="tpu_custom_call" | custom-call | flops 805306368 | bytes 3145728 | tf_op jit(solution)/shard_map/attention/pallas_call | solution.py:137
  10.4 0.5 collective-permute-start.5
  10.9 0.1 collective-permute-start.6
  11.0 1.1 %collective-permute-done.1.far_ref = bf16[128,1536]{1,0:T(8,128)(2,1)S(1)} collective-permute-done((bf16[128,1536]{1,0:T(8,128)(2,1)S(1)}, bf16[128,1536]{1,0:T(8,128)(2,1)S(1)}, u32[]{:S(2)}, u32[]{:S(2)}) %collective-permute-start.1) | collective-permute-done | bytes 393248 | tf_op jit(solution)/shard_map/ppermute | solution.py:33
  12.1 0.1 collective-permute-start.7
  12.3 0.4 norm.1
  12.6 5.3 %collective-permute-start.2 = (bf16[64,1536]{1,0:T(8,128)(2,1)S(1)}, bf16[64,1536]{1,0:T(8,128)(2,1)S(1)}, u32[]{:S(2)}, u32[]{:S(2)}) collective-permute-start(bf16[64,1536]{1,0:T(8,128)(2,1)S(1)} %get-tuple-element.39), channel_id=1, source_target_pairs={{0,16},{2,18},{4,20},{6,22},{8,24},{10,26},{12,28},{14,30},{16,0},... | collective-permute-start | bytes 589832 | tf_op jit(solution)/shard_map/ppermute | solution.py:38
  18.0 0.1 collective-permute-start.3
  18.1 1.5 %packed_rows.2 = (bf16[256,1536]{1,0:T(8,128)(2,1)}, s32[4,128]{1,0:T(4,128)S(1)}) custom-call(s32[1]{0:T(128)} %bitcast.1.base_ref, s32[1]{0:T(128)} %bitcast.side_ref, f32[8,128]{1,0:T(8,128)S(1)} %pad_maximum_fusion.1.notes_ref.weights_ref, bf16[128,1536]{1,0:T(8,128)(2,1)S(1)} %get-tuple-element.37.refs_0_), custom_call_target="tpu_custom_call" | custom-call | flops 100663296 | bytes 786432 | tf_op jit(solution)/shard_map/packed_rows/pallas_call | solution.py:209
  19.6 8.2 %collective-permute-done.3.notes_ref.weights_ref = f32[8,128]{1,0:T(8,128)S(1)} collective-permute-done((f32[8,128]{1,0:T(8,128)S(1)}, f32[8,128]{1,0:T(8,128)S(1)}, u32[]{:S(2)}, u32[]{:S(2)}) %collective-permute-start.3) | collective-permute-done | bytes 4128 | tf_op jit(solution)/shard_map/ppermute | solution.py:38
  27.8 1.4 %collective-permute-done.4.refs_1_ = bf16[64,1536]{1,0:T(8,128)(2,1)S(1)} collective-permute-done((bf16[64,1536]{1,0:T(8,128)(2,1)S(1)}, bf16[64,1536]{1,0:T(8,128)(2,1)S(1)}, u32[]{:S(2)}, u32[]{:S(2)}) %collective-permute-start.4) | collective-permute-done | bytes 196640 | tf_op jit(solution)/shard_map/ppermute | solution.py:33
  29.2 0.5 packed_rows.3
  29.7 15.9 %all_to_all.20 = bf16[8,32,1536]{2,1,0:T(8,128)(2,1)} all-to-all(bf16[8,32,1536]{2,1,0:T(8,128)(2,1)S(1)} %bitcast.16), channel_id=1, replica_groups={{0,2,4,6,8,10,12,14},{16,18,20,22,24,26,28,30},{1,3,5,7,9,11,13,15},{17..., dimensions={0} | all-to-all | bytes 1572864 | tf_op jit(solution)/shard_map/all_to_all | solution.py:403
  45.7 3.6 %all-to-all-start.1 = ((bf16[8,32,1536]{2,1,0:T(8,128)(2,1)}), bf16[8,32,1536]{2,1,0:T(8,128)(2,1)S(1)}, u32[]{:S(2)}, u32[]{:S(2)}) async-start(bf16[8,32,1536]{2,1,0:T(8,128)(2,1)} %bitcast.7), calls=%async_computation.1 | async-start | bytes 1572864 | tf_op jit(solution)/shard_map/all_to_all | solution.py:403
  49.2 8.5 %expert_layer.2 = bf16[256,1536]{1,0:T(8,128)(2,1)} custom-call(bf16[256,1536]{1,0:T(8,128)(2,1)} %bitcast.19, bf16[1,1536,768]{2,1,0:T(8,128)(2,1)} %gate_hbm.3, bf16[1,1536,768]{2,1,0:T(8,128)(2,1)} %up_hbm.3, bf16[1,768,1536]{2,1,0:T(8,128)(2,1)} %down_hbm.3, bf16[1,1536,768]{2,1,0:T(8,128)(2,1)} %collective-permute-done.5.gate_too_hbm, ...), custom_call_target="tpu_custom_call" | custom-call | flops 3623878656 | bytes 14155776 | tf_op jit(solution)/shard_map/expert_layer/pallas_call | solution.py:295
  57.7 2.5 %all-to-all-done.1 = bf16[8,32,1536]{2,1,0:T(8,128)(2,1)S(1)} async-done(((bf16[8,32,1536]{2,1,0:T(8,128)(2,1)}), bf16[8,32,1536]{2,1,0:T(8,128)(2,1)S(1)}, u32[]{:S(2)}, u32[]{:S(2)}) %all-to-all-start.1) | async-done | bytes 786464 | tf_op jit(solution)/shard_map/all_to_all | solution.py:403
  60.2 3.5 %all-to-all-start.2 = ((bf16[8,32,1536]{2,1,0:T(8,128)(2,1)}), bf16[8,32,1536]{2,1,0:T(8,128)(2,1)S(1)}, u32[]{:S(2)}, u32[]{:S(2)}) async-start(bf16[8,32,1536]{2,1,0:T(8,128)(2,1)} %bitcast.20), calls=%async_computation.2 | async-start | bytes 1572864 | tf_op jit(solution)/shard_map/all_to_all | solution.py:403
  63.8 8.5 %expert_layer.3 = bf16[256,1536]{1,0:T(8,128)(2,1)} custom-call(bf16[256,1536]{1,0:T(8,128)(2,1)} %bitcast.18, bf16[1,1536,768]{2,1,0:T(8,128)(2,1)} %gate_hbm.3, bf16[1,1536,768]{2,1,0:T(8,128)(2,1)} %up_hbm.3, bf16[1,768,1536]{2,1,0:T(8,128)(2,1)} %down_hbm.3, bf16[1,1536,768]{2,1,0:T(8,128)(2,1)} %collective-permute-done.5.gate_too_hbm, ...), custom_call_target="tpu_custom_call" | custom-call | flops 3623878656 | bytes 14155776 | tf_op jit(solution)/shard_map/expert_layer/pallas_call | solution.py:295
  72.3 2.5 %all-to-all-done.2 = bf16[8,32,1536]{2,1,0:T(8,128)(2,1)S(1)} async-done(((bf16[8,32,1536]{2,1,0:T(8,128)(2,1)}), bf16[8,32,1536]{2,1,0:T(8,128)(2,1)S(1)}, u32[]{:S(2)}, u32[]{:S(2)}) %all-to-all-start.2) | async-done | bytes 786464 | tf_op jit(solution)/shard_map/all_to_all | solution.py:403
  74.8 3.5 %all-to-all-start.3 = ((bf16[8,32,1536]{2,1,0:T(8,128)(2,1)}), bf16[8,32,1536]{2,1,0:T(8,128)(2,1)S(1)}, u32[]{:S(2)}, u32[]{:S(2)}) async-start(bf16[8,32,1536]{2,1,0:T(8,128)(2,1)} %bitcast.17), calls=%async_computation.3 | async-start | bytes 1572864 | tf_op jit(solution)/shard_map/all_to_all | solution.py:403
  78.3 0.5 combine.3
  78.9 1.4 %collective-permute-done.8 = bf16[128,768]{1,0:T(8,128)(2,1)S(1)} collective-permute-done((bf16[128,768]{1,0:T(8,128)(2,1)S(1)}, bf16[128,768]{1,0:T(8,128)(2,1)S(1)}, u32[]{:S(2)}, u32[]{:S(2)}) %collective-permute-start.8) | collective-permute-done | bytes 196640 | tf_op jit(solution)/shard_map/ppermute | solution.py:33
  80.4 1.7 %collective-permute-start.9 = (bf16[128,768]{1,0:T(8,128)(2,1)S(1)}, bf16[128,768]{1,0:T(8,128)(2,1)S(1)}, u32[]{:S(2)}, u32[]{:S(2)}) collective-permute-start(bf16[128,768]{1,0:T(8,128)(2,1)S(1)} %add_convert_fusion.1), channel_id=1, source_target_pairs={{0,16},{2,18},{4,20},{6,22},{8,24},{10,26},{12,28},{14,30},{16,0},... | collective-permute-start | bytes 589832 | tf_op jit(solution)/shard_map/ppermute | solution.py:38
  82.0 11.6 %all-to-all-done.3 = bf16[8,32,1536]{2,1,0:T(8,128)(2,1)S(1)} async-done(((bf16[8,32,1536]{2,1,0:T(8,128)(2,1)}), bf16[8,32,1536]{2,1,0:T(8,128)(2,1)S(1)}, u32[]{:S(2)}, u32[]{:S(2)}) %all-to-all-start.3) | async-done | bytes 786464 | tf_op jit(solution)/shard_map/all_to_all | solution.py:403
  93.6 0.5 combine.2
  94.2 1.4 %collective-permute-done.10 = bf16[128,768]{1,0:T(8,128)(2,1)S(1)} collective-permute-done((bf16[128,768]{1,0:T(8,128)(2,1)S(1)}, bf16[128,768]{1,0:T(8,128)(2,1)S(1)}, u32[]{:S(2)}, u32[]{:S(2)}) %collective-permute-start.10) | collective-permute-done | bytes 196640 | tf_op jit(solution)/shard_map/ppermute | solution.py:33
  95.6 0.7 add_convert_fusion
  (23 shorter events, 0.3 us)
Async XLA Ops:
  0.0 12.2 %copy-start.2 = (f32[1536]{0:T(1024)S(1)}, f32[1536]{0:T(1024)}, u32[]{:S(2)}) copy-start(f32[1536]{0:T(1024)} %param.18) | copy-start | bytes 18436
  0.0 12.3 %copy-start = (bf16[128,1536]{1,0:T(8,128)(2,1)S(1)}, bf16[128,1536]{1,0:T(8,128)(2,1)}, u32[]{:S(2)}) copy-start(bf16[128,1536]{1,0:T(8,128)(2,1)} %residual_ref.1) | copy-start | bytes 1179652
  0.8 6.7 %collective-permute-start = (bf16[128,256]{1,0:T(8,128)(2,1)S(1)}, bf16[128,256]{1,0:T(8,128)(2,1)S(1)}, u32[]{:S(2)}, u32[]{:S(2)}) collective-permute-start(bf16[128,256]{1,0:T(8,128)(2,1)S(1)} %pad_maximum_fusion.kv_ref), channel_id=1, source_target_pairs={{0,2},{2,4},{4,6},{6,8},{8,10},{10,12},{12,14},{14,16},{16,18},{18... | collective-permute-start | bytes 196616 | tf_op jit(solution)/shard_map/ppermute | solution.py:28
  7.6 10.4 %copy-start.3 = (s32[128,4]{0,1:T(4,128)S(1)}, s32[128,4]{0,1:T(4,128)}, u32[]{:S(2)}) copy-start(s32[128,4]{0,1:T(4,128)} %param.19) | copy-start | bytes 6148
  7.6 10.4 %copy-start.4 = (f32[128,4]{0,1:T(4,128)S(1)}, f32[128,4]{0,1:T(4,128)}, u32[]{:S(2)}) copy-start(f32[128,4]{0,1:T(4,128)} %param.20) | copy-start | bytes 6148
  10.3 1.8 %collective-permute-start.1 = (bf16[128,1536]{1,0:T(8,128)(2,1)S(1)}, bf16[128,1536]{1,0:T(8,128)(2,1)S(1)}, u32[]{:S(2)}, u32[]{:S(2)}) collective-permute-start(bf16[128,1536]{1,0:T(8,128)(2,1)S(1)} %attention.1.near_ref), channel_id=1, source_target_pairs={{0,1},{1,0},{2,3},{3,2},{4,5},{5,4},{6,7},{7,6},{8,9},{9,8},{10,11... | collective-permute-start | bytes 1179656 | tf_op jit(solution)/shard_map/ppermute | solution.py:33
  10.4 35.3 %collective-permute-start.5 = (bf16[1,1536,768]{2,1,0:T(8,128)(2,1)}, bf16[1,1536,768]{2,1,0:T(8,128)(2,1)}, u32[]{:S(2)}, u32[]{:S(2)}) collective-permute-start(bf16[1,1536,768]{2,1,0:T(8,128)(2,1)} %gate_hbm.3), channel_id=1, source_target_pairs={{0,1},{1,0},{2,3},{3,2},{4,5},{5,4},{6,7},{7,6},{8,9},{9,8},{10,11... | collective-permute-start | bytes 7077896 | tf_op jit(solution)/shard_map/ppermute | solution.py:33
  10.9 34.8 %collective-permute-start.6 = (bf16[1,1536,768]{2,1,0:T(8,128)(2,1)}, bf16[1,1536,768]{2,1,0:T(8,128)(2,1)}, u32[]{:S(2)}, u32[]{:S(2)}) collective-permute-start(bf16[1,1536,768]{2,1,0:T(8,128)(2,1)} %up_hbm.3), channel_id=1, source_target_pairs={{0,1},{1,0},{2,3},{3,2},{4,5},{5,4},{6,7},{7,6},{8,9},{9,8},{10,11... | collective-permute-start | bytes 7077896 | tf_op jit(solution)/shard_map/ppermute | solution.py:33
  12.1 33.6 %collective-permute-start.7 = (bf16[1,768,1536]{2,1,0:T(8,128)(2,1)}, bf16[1,768,1536]{2,1,0:T(8,128)(2,1)}, u32[]{:S(2)}, u32[]{:S(2)}) collective-permute-start(bf16[1,768,1536]{2,1,0:T(8,128)(2,1)} %down_hbm.3), channel_id=1, source_target_pairs={{0,1},{1,0},{2,3},{3,2},{4,5},{5,4},{6,7},{7,6},{8,9},{9,8},{10,11... | collective-permute-start | bytes 7077896 | tf_op jit(solution)/shard_map/ppermute | solution.py:33
  12.6 15.1 %collective-permute-start.2 = (bf16[64,1536]{1,0:T(8,128)(2,1)S(1)}, bf16[64,1536]{1,0:T(8,128)(2,1)S(1)}, u32[]{:S(2)}, u32[]{:S(2)}) collective-permute-start(bf16[64,1536]{1,0:T(8,128)(2,1)S(1)} %get-tuple-element.39), channel_id=1, source_target_pairs={{0,16},{2,18},{4,20},{6,22},{8,24},{10,26},{12,28},{14,30},{16,0},... | collective-permute-start | bytes 589832 | tf_op jit(solution)/shard_map/ppermute | solution.py:38
  18.0 9.8 %collective-permute-start.3 = (f32[8,128]{1,0:T(8,128)S(1)}, f32[8,128]{1,0:T(8,128)S(1)}, u32[]{:S(2)}, u32[]{:S(2)}) collective-permute-start(f32[8,128]{1,0:T(8,128)S(1)} %pad_maximum_fusion.1.notes_ref.weights_ref), channel_id=1, source_target_pairs={{0,16},{2,18},{4,20},{6,22},{8,24},{10,26},{12,28},{14,30},{16,0},... | collective-permute-start | bytes 12296 | tf_op jit(solution)/shard_map/ppermute | solution.py:38
  27.8 1.4 %collective-permute-start.4 = (bf16[64,1536]{1,0:T(8,128)(2,1)S(1)}, bf16[64,1536]{1,0:T(8,128)(2,1)S(1)}, u32[]{:S(2)}, u32[]{:S(2)}) collective-permute-start(bf16[64,1536]{1,0:T(8,128)(2,1)S(1)} %collective-permute-done.2.refs_0_), channel_id=1, source_target_pairs={{0,1},{1,0},{2,3},{3,2},{4,5},{5,4},{6,7},{7,6},{8,9},{9,8},{10,11... | collective-permute-start | bytes 589832 | tf_op jit(solution)/shard_map/ppermute | solution.py:33
  45.7 14.5 %all-to-all-start.1 = ((bf16[8,32,1536]{2,1,0:T(8,128)(2,1)}), bf16[8,32,1536]{2,1,0:T(8,128)(2,1)S(1)}, u32[]{:S(2)}, u32[]{:S(2)}) async-start(bf16[8,32,1536]{2,1,0:T(8,128)(2,1)} %bitcast.7), calls=%async_computation.1 | async-start | bytes 1572864 | tf_op jit(solution)/shard_map/all_to_all | solution.py:403
  60.2 3.6 %copy-start.1 = (bf16[8,32,1536]{2,1,0:T(8,128)(2,1)}, bf16[8,32,1536]{2,1,0:T(8,128)(2,1)S(1)}, u32[]{:S(2)}) copy-start(bf16[8,32,1536]{2,1,0:T(8,128)(2,1)S(1)} %all-to-all-done.1) | copy-start | bytes 2359300
  60.2 14.6 %all-to-all-start.2 = ((bf16[8,32,1536]{2,1,0:T(8,128)(2,1)}), bf16[8,32,1536]{2,1,0:T(8,128)(2,1)S(1)}, u32[]{:S(2)}, u32[]{:S(2)}) async-start(bf16[8,32,1536]{2,1,0:T(8,128)(2,1)} %bitcast.20), calls=%async_computation.2 | async-start | bytes 1572864 | tf_op jit(solution)/shard_map/all_to_all | solution.py:403
  74.8 18.8 %all-to-all-start.3 = ((bf16[8,32,1536]{2,1,0:T(8,128)(2,1)}), bf16[8,32,1536]{2,1,0:T(8,128)(2,1)S(1)}, u32[]{:S(2)}, u32[]{:S(2)}) async-start(bf16[8,32,1536]{2,1,0:T(8,128)(2,1)} %bitcast.17), calls=%async_computation.3 | async-start | bytes 1572864 | tf_op jit(solution)/shard_map/all_to_all | solution.py:403
  78.8 1.5 %collective-permute-start.8 = (bf16[128,768]{1,0:T(8,128)(2,1)S(1)}, bf16[128,768]{1,0:T(8,128)(2,1)S(1)}, u32[]{:S(2)}, u32[]{:S(2)}) collective-permute-start(bf16[128,768]{1,0:T(8,128)(2,1)S(1)} %get-tuple-element.60), channel_id=1, source_target_pairs={{0,1},{1,0},{2,3},{3,2},{4,5},{5,4},{6,7},{7,6},{8,9},{9,8},{10,11... | collective-permute-start | bytes 589832 | tf_op jit(solution)/shard_map/ppermute | solution.py:33
  80.4 13.7 %collective-permute-start.9 = (bf16[128,768]{1,0:T(8,128)(2,1)S(1)}, bf16[128,768]{1,0:T(8,128)(2,1)S(1)}, u32[]{:S(2)}, u32[]{:S(2)}) collective-permute-start(bf16[128,768]{1,0:T(8,128)(2,1)S(1)} %add_convert_fusion.1), channel_id=1, source_target_pairs={{0,16},{2,18},{4,20},{6,22},{8,24},{10,26},{12,28},{14,30},{16,0},... | collective-permute-start | bytes 589832 | tf_op jit(solution)/shard_map/ppermute | solution.py:38
  94.1 1.5 %collective-permute-start.10 = (bf16[128,768]{1,0:T(8,128)(2,1)S(1)}, bf16[128,768]{1,0:T(8,128)(2,1)S(1)}, u32[]{:S(2)}, u32[]{:S(2)}) collective-permute-start(bf16[128,768]{1,0:T(8,128)(2,1)S(1)} %get-tuple-element.61), channel_id=1, source_target_pairs={{0,1},{1,0},{2,3},{3,2},{4,5},{5,4},{6,7},{7,6},{8,9},{9,8},{10,11... | collective-permute-start | bytes 589832 | tf_op jit(solution)/shard_map/ppermute | solution.py:33

commit v4 on v1

--- a/solution.py
+++ b/solution.py
@@ -427,7 +427,6 @@
     summed_peer = (mine_peer + swapped(sent_peer, "tp").astype(jnp.float32)).astype(jnp.bfloat16)
     back = swapped_halves(summed_peer, "seq")
     mine, sent = combine(side, placed, notes, returned, half, (kept,))
-    sent, back = lax.optimization_barrier((sent, back))
     return (mine + swapped(sent, "tp").astype(jnp.float32) + back.astype(jnp.float32)).astype(jnp.bfloat16)
 
 

time: 96.9 us -> 96.9 us (level)
  no operation moved by 1% of the time
where the time goes in v4:
time: 96.9 us; the launch traced here: 96.3 us
  waiting for transfers between devices  30.3 us (31%)
  starting transfers between devices  23.5 us (24%)
  Pallas kernels  23.1 us (24%)
  blocking collectives  15.9 us (16%)
  other arithmetic  2.61 us (3%)
    pallas_call x2, Pallas kernels, expert_layer(): pl.pallas_call(expert_kernel, out_shape=shape_of((rows, width)), in_specs...  17 us
    all_to_all x3, waiting for transfers between devices, exchanged(): lax.all_to_all(block, 'seq', split_axis=0, concat_axis=0, axis_index_grou...  16.5 us
    all_to_all x1, blocking collectives, exchanged(): lax.all_to_all(block, 'seq', split_axis=0, concat_axis=0, axis_index_grou...  15.9 us
    all_to_all x3, starting transfers between devices, exchanged(): lax.all_to_all(block, 'seq', split_axis=0, concat_axis=0, axis_index_grou...  10.7 us
    ppermute x3, waiting for transfers between devices, swapped_halves(): lax.ppermute(block, axis, [(i, (i + count // 2) % count) for i in range(c...  8.22 us
    ppermute x3, starting transfers between devices, swapped_halves(): lax.ppermute(block, axis, [(i, (i + count // 2) % count) for i in range(c...  7.1 us
    ppermute x7, waiting for transfers between devices, swapped(): return lax.ppermute(block, axis, [(i, count - 1 - i) for i in range(count)])  5.43 us
    ppermute x1, starting transfers between devices, passed_along(): return lax.ppermute(block, axis, route)  4.84 us
  transfers between devices with their start and end apart: 14, of which 9 were waited for; matrix products, arithmetic and copies ran while one was open for 2% of the time, Pallas kernels for 21%

profile of v4, /device:TPU:0, one launch (start us, length us, event | category | flops | bytes accessed | tf_op | source)
XLA Modules:
  0.0 96.3 jit_solution(8003902061384592578)
XLA Ops:
  0.0 0.8 pad_maximum_fusion.kv_ref
  0.8 4.8 %collective-permute-start = (bf16[128,256]{1,0:T(8,128)(2,1)S(1)}, bf16[128,256]{1,0:T(8,128)(2,1)S(1)}, u32[]{:S(2)}, u32[]{:S(2)}) collective-permute-start(bf16[128,256]{1,0:T(8,128)(2,1)S(1)} %pad_maximum_fusion.kv_ref), channel_id=1, source_target_pairs={{0,2},{2,4},{4,6},{6,8},{8,10},{10,12},{12,14},{14,16},{16,18},{18... | collective-permute-start | bytes 196616 | tf_op jit(solution)/shard_map/ppermute | solution.py:28
  5.7 0.7 broadcast_in_dim.2.sink_ref
  6.4 1.0 %broadcast_multiply_fusion.q_ref = bf16[128,1024]{1,0:T(8,128)(2,1)S(1)} fusion(bf16[128,1024]{1,0:T(8,128)(2,1)} %param.13), kind=kLoop, calls=%fused_computation.2 | loop fusion | flops 131072 | bytes 524288 | tf_op jit(solution)/shard_map/mul | solution.py:390
  7.4 0.2 collective-permute-done.before_ref
  7.6 2.7 %attention.1.near_ref = bf16[128,1536]{1,0:T(8,128)(2,1)S(1)} custom-call(s32[1]{0:T(128)} %bitcast.4.first_ref, f32[16,128]{1,0:T(8,128)S(1)} %broadcast_in_dim.2.sink_ref, bf16[128,1024]{1,0:T(8,128)(2,1)S(1)} %broadcast_multiply_fusion.q_ref, bf16[128,256]{1,0:T(8,128)(2,1)S(1)} %pad_maximum_fusion.kv_ref, ...), custom_call_target="tpu_custom_call" | custom-call | flops 805306368 | bytes 3145728 | tf_op jit(solution)/shard_map/attention/pallas_call | solution.py:137
  10.4 0.5 collective-permute-start.5
  10.9 0.1 collective-permute-start.6
  11.0 1.1 %collective-permute-done.1.far_ref = bf16[128,1536]{1,0:T(8,128)(2,1)S(1)} collective-permute-done((bf16[128,1536]{1,0:T(8,128)(2,1)S(1)}, bf16[128,1536]{1,0:T(8,128)(2,1)S(1)}, u32[]{:S(2)}, u32[]{:S(2)}) %collective-permute-start.1) | collective-permute-done | bytes 393248 | tf_op jit(solution)/shard_map/ppermute | solution.py:33
  12.1 0.1 collective-permute-start.7
  12.3 0.4 norm.1
  12.6 5.3 %collective-permute-start.2 = (bf16[64,1536]{1,0:T(8,128)(2,1)S(1)}, bf16[64,1536]{1,0:T(8,128)(2,1)S(1)}, u32[]{:S(2)}, u32[]{:S(2)}) collective-permute-start(bf16[64,1536]{1,0:T(8,128)(2,1)S(1)} %get-tuple-element.37), channel_id=1, source_target_pairs={{0,16},{2,18},{4,20},{6,22},{8,24},{10,26},{12,28},{14,30},{16,0},... | collective-permute-start | bytes 589832 | tf_op jit(solution)/shard_map/ppermute | solution.py:38
  18.0 0.1 collective-permute-start.3
  18.1 1.5 %packed_rows.2 = (bf16[256,1536]{1,0:T(8,128)(2,1)}, s32[4,128]{1,0:T(4,128)S(1)}) custom-call(s32[1]{0:T(128)} %bitcast.1.base_ref, s32[1]{0:T(128)} %bitcast.side_ref, f32[8,128]{1,0:T(8,128)S(1)} %pad_maximum_fusion.1.notes_ref.weights_ref, bf16[128,1536]{1,0:T(8,128)(2,1)S(1)} %get-tuple-element.35.refs_0_), custom_call_target="tpu_custom_call" | custom-call | flops 100663296 | bytes 786432 | tf_op jit(solution)/shard_map/packed_rows/pallas_call | solution.py:209
  19.6 8.2 %collective-permute-done.3.notes_ref.weights_ref = f32[8,128]{1,0:T(8,128)S(1)} collective-permute-done((f32[8,128]{1,0:T(8,128)S(1)}, f32[8,128]{1,0:T(8,128)S(1)}, u32[]{:S(2)}, u32[]{:S(2)}) %collective-permute-start.3) | collective-permute-done | bytes 4128 | tf_op jit(solution)/shard_map/ppermute | solution.py:38
  27.8 1.4 %collective-permute-done.4.refs_1_ = bf16[64,1536]{1,0:T(8,128)(2,1)S(1)} collective-permute-done((bf16[64,1536]{1,0:T(8,128)(2,1)S(1)}, bf16[64,1536]{1,0:T(8,128)(2,1)S(1)}, u32[]{:S(2)}, u32[]{:S(2)}) %collective-permute-start.4) | collective-permute-done | bytes 196640 | tf_op jit(solution)/shard_map/ppermute | solution.py:33
  29.2 0.5 packed_rows.3
  29.7 15.9 %all_to_all.20 = bf16[8,32,1536]{2,1,0:T(8,128)(2,1)} all-to-all(bf16[8,32,1536]{2,1,0:T(8,128)(2,1)S(1)} %bitcast.16), channel_id=1, replica_groups={{0,2,4,6,8,10,12,14},{16,18,20,22,24,26,28,30},{1,3,5,7,9,11,13,15},{17..., dimensions={0} | all-to-all | bytes 1572864 | tf_op jit(solution)/shard_map/all_to_all | solution.py:403
  45.7 3.6 %all-to-all-start.1 = ((bf16[8,32,1536]{2,1,0:T(8,128)(2,1)}), bf16[8,32,1536]{2,1,0:T(8,128)(2,1)S(1)}, u32[]{:S(2)}, u32[]{:S(2)}) async-start(bf16[8,32,1536]{2,1,0:T(8,128)(2,1)} %bitcast.7), calls=%async_computation.1 | async-start | bytes 1572864 | tf_op jit(solution)/shard_map/all_to_all | solution.py:403
  49.2 8.5 %expert_layer.2 = bf16[256,1536]{1,0:T(8,128)(2,1)} custom-call(bf16[256,1536]{1,0:T(8,128)(2,1)} %bitcast.19, bf16[1,1536,768]{2,1,0:T(8,128)(2,1)} %gate_hbm.3, bf16[1,1536,768]{2,1,0:T(8,128)(2,1)} %up_hbm.3, bf16[1,768,1536]{2,1,0:T(8,128)(2,1)} %down_hbm.3, bf16[1,1536,768]{2,1,0:T(8,128)(2,1)} %collective-permute-done.5.gate_too_hbm, ...), custom_call_target="tpu_custom_call" | custom-call | flops 3623878656 | bytes 14155776 | tf_op jit(solution)/shard_map/expert_layer/pallas_call | solution.py:295
  57.7 2.5 %all-to-all-done.1 = bf16[8,32,1536]{2,1,0:T(8,128)(2,1)S(1)} async-done(((bf16[8,32,1536]{2,1,0:T(8,128)(2,1)}), bf16[8,32,1536]{2,1,0:T(8,128)(2,1)S(1)}, u32[]{:S(2)}, u32[]{:S(2)}) %all-to-all-start.1) | async-done | bytes 786464 | tf_op jit(solution)/shard_map/all_to_all | solution.py:403
  60.2 3.5 %all-to-all-start.2 = ((bf16[8,32,1536]{2,1,0:T(8,128)(2,1)}), bf16[8,32,1536]{2,1,0:T(8,128)(2,1)S(1)}, u32[]{:S(2)}, u32[]{:S(2)}) async-start(bf16[8,32,1536]{2,1,0:T(8,128)(2,1)} %bitcast.20), calls=%async_computation.2 | async-start | bytes 1572864 | tf_op jit(solution)/shard_map/all_to_all | solution.py:403
  63.8 8.5 %expert_layer.3 = bf16[256,1536]{1,0:T(8,128)(2,1)} custom-call(bf16[256,1536]{1,0:T(8,128)(2,1)} %bitcast.18, bf16[1,1536,768]{2,1,0:T(8,128)(2,1)} %gate_hbm.3, bf16[1,1536,768]{2,1,0:T(8,128)(2,1)} %up_hbm.3, bf16[1,768,1536]{2,1,0:T(8,128)(2,1)} %down_hbm.3, bf16[1,1536,768]{2,1,0:T(8,128)(2,1)} %collective-permute-done.5.gate_too_hbm, ...), custom_call_target="tpu_custom_call" | custom-call | flops 3623878656 | bytes 14155776 | tf_op jit(solution)/shard_map/expert_layer/pallas_call | solution.py:295
  72.3 2.5 %all-to-all-done.2 = bf16[8,32,1536]{2,1,0:T(8,128)(2,1)S(1)} async-done(((bf16[8,32,1536]{2,1,0:T(8,128)(2,1)}), bf16[8,32,1536]{2,1,0:T(8,128)(2,1)S(1)}, u32[]{:S(2)}, u32[]{:S(2)}) %all-to-all-start.2) | async-done | bytes 786464 | tf_op jit(solution)/shard_map/all_to_all | solution.py:403
  74.8 3.5 %all-to-all-start.3 = ((bf16[8,32,1536]{2,1,0:T(8,128)(2,1)}), bf16[8,32,1536]{2,1,0:T(8,128)(2,1)S(1)}, u32[]{:S(2)}, u32[]{:S(2)}) async-start(bf16[8,32,1536]{2,1,0:T(8,128)(2,1)} %bitcast.17), calls=%async_computation.3 | async-start | bytes 1572864 | tf_op jit(solution)/shard_map/all_to_all | solution.py:403
  78.3 0.5 combine.3
  78.9 1.4 %collective-permute-done.9 = bf16[128,768]{1,0:T(8,128)(2,1)S(1)} collective-permute-done((bf16[128,768]{1,0:T(8,128)(2,1)S(1)}, bf16[128,768]{1,0:T(8,128)(2,1)S(1)}, u32[]{:S(2)}, u32[]{:S(2)}) %collective-permute-start.9) | collective-permute-done | bytes 196640 | tf_op jit(solution)/shard_map/ppermute | solution.py:33
  80.4 1.7 %collective-permute-start.10 = (bf16[128,768]{1,0:T(8,128)(2,1)S(1)}, bf16[128,768]{1,0:T(8,128)(2,1)S(1)}, u32[]{:S(2)}, u32[]{:S(2)}) collective-permute-start(bf16[128,768]{1,0:T(8,128)(2,1)S(1)} %add_convert_fusion.1), channel_id=1, source_target_pairs={{0,16},{2,18},{4,20},{6,22},{8,24},{10,26},{12,28},{14,30},{16,0},... | collective-permute-start | bytes 589832 | tf_op jit(solution)/shard_map/ppermute | solution.py:38
  82.0 11.6 %all-to-all-done.3 = bf16[8,32,1536]{2,1,0:T(8,128)(2,1)S(1)} async-done(((bf16[8,32,1536]{2,1,0:T(8,128)(2,1)}), bf16[8,32,1536]{2,1,0:T(8,128)(2,1)S(1)}, u32[]{:S(2)}, u32[]{:S(2)}) %all-to-all-start.3) | async-done | bytes 786464 | tf_op jit(solution)/shard_map/all_to_all | solution.py:403
  93.6 0.5 combine.2
  94.2 1.4 %collective-permute-done.8 = bf16[128,768]{1,0:T(8,128)(2,1)S(1)} collective-permute-done((bf16[128,768]{1,0:T(8,128)(2,1)S(1)}, bf16[128,768]{1,0:T(8,128)(2,1)S(1)}, u32[]{:S(2)}, u32[]{:S(2)}) %collective-permute-start.8) | collective-permute-done | bytes 196640 | tf_op jit(solution)/shard_map/ppermute | solution.py:33
  95.6 0.7 add_convert_fusion
  (23 shorter events, 0.3 us)
Async XLA Ops:
  0.0 12.2 %copy-start.2 = (f32[1536]{0:T(1024)S(1)}, f32[1536]{0:T(1024)}, u32[]{:S(2)}) copy-start(f32[1536]{0:T(1024)} %param.18) | copy-start | bytes 18436
  0.0 12.3 %copy-start = (bf16[128,1536]{1,0:T(8,128)(2,1)S(1)}, bf16[128,1536]{1,0:T(8,128)(2,1)}, u32[]{:S(2)}) copy-start(bf16[128,1536]{1,0:T(8,128)(2,1)} %residual_ref.1) | copy-start | bytes 1179652
  0.8 6.7 %collective-permute-start = (bf16[128,256]{1,0:T(8,128)(2,1)S(1)}, bf16[128,256]{1,0:T(8,128)(2,1)S(1)}, u32[]{:S(2)}, u32[]{:S(2)}) collective-permute-start(bf16[128,256]{1,0:T(8,128)(2,1)S(1)} %pad_maximum_fusion.kv_ref), channel_id=1, source_target_pairs={{0,2},{2,4},{4,6},{6,8},{8,10},{10,12},{12,14},{14,16},{16,18},{18... | collective-permute-start | bytes 196616 | tf_op jit(solution)/shard_map/ppermute | solution.py:28
  7.6 10.4 %copy-start.3 = (s32[128,4]{0,1:T(4,128)S(1)}, s32[128,4]{0,1:T(4,128)}, u32[]{:S(2)}) copy-start(s32[128,4]{0,1:T(4,128)} %param.19) | copy-start | bytes 6148
  7.6 10.4 %copy-start.4 = (f32[128,4]{0,1:T(4,128)S(1)}, f32[128,4]{0,1:T(4,128)}, u32[]{:S(2)}) copy-start(f32[128,4]{0,1:T(4,128)} %param.20) | copy-start | bytes 6148
  10.3 1.8 %collective-permute-start.1 = (bf16[128,1536]{1,0:T(8,128)(2,1)S(1)}, bf16[128,1536]{1,0:T(8,128)(2,1)S(1)}, u32[]{:S(2)}, u32[]{:S(2)}) collective-permute-start(bf16[128,1536]{1,0:T(8,128)(2,1)S(1)} %attention.1.near_ref), channel_id=1, source_target_pairs={{0,1},{1,0},{2,3},{3,2},{4,5},{5,4},{6,7},{7,6},{8,9},{9,8},{10,11... | collective-permute-start | bytes 1179656 | tf_op jit(solution)/shard_map/ppermute | solution.py:33
  10.4 35.3 %collective-permute-start.5 = (bf16[1,1536,768]{2,1,0:T(8,128)(2,1)}, bf16[1,1536,768]{2,1,0:T(8,128)(2,1)}, u32[]{:S(2)}, u32[]{:S(2)}) collective-permute-start(bf16[1,1536,768]{2,1,0:T(8,128)(2,1)} %gate_hbm.3), channel_id=1, source_target_pairs={{0,1},{1,0},{2,3},{3,2},{4,5},{5,4},{6,7},{7,6},{8,9},{9,8},{10,11... | collective-permute-start | bytes 7077896 | tf_op jit(solution)/shard_map/ppermute | solution.py:33
  10.9 34.8 %collective-permute-start.6 = (bf16[1,1536,768]{2,1,0:T(8,128)(2,1)}, bf16[1,1536,768]{2,1,0:T(8,128)(2,1)}, u32[]{:S(2)}, u32[]{:S(2)}) collective-permute-start(bf16[1,1536,768]{2,1,0:T(8,128)(2,1)} %up_hbm.3), channel_id=1, source_target_pairs={{0,1},{1,0},{2,3},{3,2},{4,5},{5,4},{6,7},{7,6},{8,9},{9,8},{10,11... | collective-permute-start | bytes 7077896 | tf_op jit(solution)/shard_map/ppermute | solution.py:33
  12.1 33.6 %collective-permute-start.7 = (bf16[1,768,1536]{2,1,0:T(8,128)(2,1)}, bf16[1,768,1536]{2,1,0:T(8,128)(2,1)}, u32[]{:S(2)}, u32[]{:S(2)}) collective-permute-start(bf16[1,768,1536]{2,1,0:T(8,128)(2,1)} %down_hbm.3), channel_id=1, source_target_pairs={{0,1},{1,0},{2,3},{3,2},{4,5},{5,4},{6,7},{7,6},{8,9},{9,8},{10,11... | collective-permute-start | bytes 7077896 | tf_op jit(solution)/shard_map/ppermute | solution.py:33
  12.6 15.1 %collective-permute-start.2 = (bf16[64,1536]{1,0:T(8,128)(2,1)S(1)}, bf16[64,1536]{1,0:T(8,128)(2,1)S(1)}, u32[]{:S(2)}, u32[]{:S(2)}) collective-permute-start(bf16[64,1536]{1,0:T(8,128)(2,1)S(1)} %get-tuple-element.37), channel_id=1, source_target_pairs={{0,16},{2,18},{4,20},{6,22},{8,24},{10,26},{12,28},{14,30},{16,0},... | collective-permute-start | bytes 589832 | tf_op jit(solution)/shard_map/ppermute | solution.py:38
  18.0 9.8 %collective-permute-start.3 = (f32[8,128]{1,0:T(8,128)S(1)}, f32[8,128]{1,0:T(8,128)S(1)}, u32[]{:S(2)}, u32[]{:S(2)}) collective-permute-start(f32[8,128]{1,0:T(8,128)S(1)} %pad_maximum_fusion.1.notes_ref.weights_ref), channel_id=1, source_target_pairs={{0,16},{2,18},{4,20},{6,22},{8,24},{10,26},{12,28},{14,30},{16,0},... | collective-permute-start | bytes 12296 | tf_op jit(solution)/shard_map/ppermute | solution.py:38
  27.8 1.4 %collective-permute-start.4 = (bf16[64,1536]{1,0:T(8,128)(2,1)S(1)}, bf16[64,1536]{1,0:T(8,128)(2,1)S(1)}, u32[]{:S(2)}, u32[]{:S(2)}) collective-permute-start(bf16[64,1536]{1,0:T(8,128)(2,1)S(1)} %collective-permute-done.2.refs_0_), channel_id=1, source_target_pairs={{0,1},{1,0},{2,3},{3,2},{4,5},{5,4},{6,7},{7,6},{8,9},{9,8},{10,11... | collective-permute-start | bytes 589832 | tf_op jit(solution)/shard_map/ppermute | solution.py:33
  45.7 14.5 %all-to-all-start.1 = ((bf16[8,32,1536]{2,1,0:T(8,128)(2,1)}), bf16[8,32,1536]{2,1,0:T(8,128)(2,1)S(1)}, u32[]{:S(2)}, u32[]{:S(2)}) async-start(bf16[8,32,1536]{2,1,0:T(8,128)(2,1)} %bitcast.7), calls=%async_computation.1 | async-start | bytes 1572864 | tf_op jit(solution)/shard_map/all_to_all | solution.py:403
  60.2 3.6 %copy-start.1 = (bf16[8,32,1536]{2,1,0:T(8,128)(2,1)}, bf16[8,32,1536]{2,1,0:T(8,128)(2,1)S(1)}, u32[]{:S(2)}) copy-start(bf16[8,32,1536]{2,1,0:T(8,128)(2,1)S(1)} %all-to-all-done.1) | copy-start | bytes 2359300
  60.2 14.6 %all-to-all-start.2 = ((bf16[8,32,1536]{2,1,0:T(8,128)(2,1)}), bf16[8,32,1536]{2,1,0:T(8,128)(2,1)S(1)}, u32[]{:S(2)}, u32[]{:S(2)}) async-start(bf16[8,32,1536]{2,1,0:T(8,128)(2,1)} %bitcast.20), calls=%async_computation.2 | async-start | bytes 1572864 | tf_op jit(solution)/shard_map/all_to_all | solution.py:403
  74.8 18.8 %all-to-all-start.3 = ((bf16[8,32,1536]{2,1,0:T(8,128)(2,1)}), bf16[8,32,1536]{2,1,0:T(8,128)(2,1)S(1)}, u32[]{:S(2)}, u32[]{:S(2)}) async-start(bf16[8,32,1536]{2,1,0:T(8,128)(2,1)} %bitcast.17), calls=%async_computation.3 | async-start | bytes 1572864 | tf_op jit(solution)/shard_map/all_to_all | solution.py:403
  78.8 1.5 %collective-permute-start.9 = (bf16[128,768]{1,0:T(8,128)(2,1)S(1)}, bf16[128,768]{1,0:T(8,128)(2,1)S(1)}, u32[]{:S(2)}, u32[]{:S(2)}) collective-permute-start(bf16[128,768]{1,0:T(8,128)(2,1)S(1)} %get-tuple-element.58), channel_id=1, source_target_pairs={{0,1},{1,0},{2,3},{3,2},{4,5},{5,4},{6,7},{7,6},{8,9},{9,8},{10,11... | collective-permute-start | bytes 589832 | tf_op jit(solution)/shard_map/ppermute | solution.py:33
  80.4 13.8 %collective-permute-start.10 = (bf16[128,768]{1,0:T(8,128)(2,1)S(1)}, bf16[128,768]{1,0:T(8,128)(2,1)S(1)}, u32[]{:S(2)}, u32[]{:S(2)}) collective-permute-start(bf16[128,768]{1,0:T(8,128)(2,1)S(1)} %add_convert_fusion.1), channel_id=1, source_target_pairs={{0,16},{2,18},{4,20},{6,22},{8,24},{10,26},{12,28},{14,30},{16,0},... | collective-permute-start | bytes 589832 | tf_op jit(solution)/shard_map/ppermute | solution.py:38
  94.1 1.5 %collective-permute-start.8 = (bf16[128,768]{1,0:T(8,128)(2,1)S(1)}, bf16[128,768]{1,0:T(8,128)(2,1)S(1)}, u32[]{:S(2)}, u32[]{:S(2)}) collective-permute-start(bf16[128,768]{1,0:T(8,128)(2,1)S(1)} %get-tuple-element.54), channel_id=1, source_target_pairs={{0,1},{1,0},{2,3},{3,2},{4,5},{5,4},{6,7},{7,6},{8,9},{9,8},{10,11... | collective-permute-start | bytes 589832 | tf_op jit(solution)/shard_map/ppermute | solution.py:33
